TPU v7x, 128 devices: a whole 4x4x4 slice. The times are simulated.
128 devices in a mesh: shard: 8 (over x_hi, z), rep: 16 (over x_lo, y, core).
Axes of the slice: x: 4 (x_hi: 2, x_lo: 2; x = x_hi * 2 + x_lo), y: 4, z: 4, core: 2. Of those that a mesh axis runs over, the one named last changes fastest.
Arguments:
- inputs: bfloat16 [16, 1024, 2048], P('rep', 'shard'), may hold values from -6 to 6
- cotangent: bfloat16 [16, 1024, 2048], P('rep', 'shard'), may hold values from -6 to 6
- ln1_gain: bfloat16 [2048], P('shard'), may hold values from 0.25 to 1.75
- ln1_bias: bfloat16 [2048], P('shard'), may hold values from -1.75 to 1.75
- qkv_weight: bfloat16 [2048, 6144], P('shard'), may hold values from -0.125 to 0.125
- qkv_bias: bfloat16 [6144], P('shard'), may hold values from -1.75 to 1.75
- out_weight: bfloat16 [2048, 2048], P('shard'), may hold values from -3 to 3
- ln2_gain: bfloat16 [2048], P('shard'), may hold values from 0.25 to 1.75
- ln2_bias: bfloat16 [2048], P('shard'), may hold values from -1.75 to 1.75
- gate_weight: bfloat16 [2048, 5632], P('shard'), may hold values from -0.125 to 0.125
- up_weight: bfloat16 [2048, 5632], P('shard'), may hold values from -0.125 to 0.125
- down_weight: bfloat16 [5632, 2048], P('shard'), may hold values from -0.078125 to 0.078125
Outputs:
- activations: bfloat16 [16, 1024, 2048], P('rep', 'shard')
- input_grad: float32 [16, 1024, 2048], P('rep', 'shard')
- ln1_gain_grad: float32 [2048], P('shard')
- ln1_bias_grad: float32 [2048], P('shard')
- qkv_weight_grad: float32 [2048, 6144], P('shard')
- qkv_bias_grad: float32 [6144], P('shard')
- out_weight_grad: float32 [2048, 2048], P('shard')
- ln2_gain_grad: float32 [2048], P('shard')
- ln2_bias_grad: float32 [2048], P('shard')
- gate_weight_grad: float32 [2048, 5632], P('shard')
- up_weight_grad: float32 [2048, 5632], P('shard')
- down_weight_grad: float32 [5632, 2048], P('shard')
All inputs are finite; a program needn't handle non-finite values.
Results may differ from a plain program's by a relative error of at most 0.025.
Values may be sent and summed in bfloat16 or wider, within the bound.
A program may use at most 384 MiB of HBM per device.

v0:
```python
import jax
import jax.numpy as jnp
from jax import lax
from jax.sharding import PartitionSpec as P

HEADS = 32
HEAD_DIM = 64
ROT = 16


EPS = 1e-05
BASE = 10000.0


def normalize(values, gain, shift):
    center = values - jnp.mean(values, -1, keepdims=True)
    inverse = lax.rsqrt(jnp.mean(center * center, -1, keepdims=True) + EPS)
    scaled = center * inverse
    return (scaled * gain.astype(jnp.float32) + shift.astype(jnp.float32), scaled, inverse)


def normalize_back(grad, gain, scaled, inverse):
    weighted = grad * gain.astype(jnp.float32)
    return inverse * (
        weighted
        - jnp.mean(weighted, -1, keepdims=True)
        - scaled * jnp.mean(weighted * scaled, -1, keepdims=True)
    )


def rotary_tables(first, length):
    positions = (first + jnp.arange(length, dtype=jnp.int32)).astype(jnp.float32)
    freqs = BASE ** (-jnp.arange(0, ROT, 2).astype(jnp.float32) / ROT)
    angles = positions[:, None] * freqs[None, :]
    angles = jnp.concatenate([angles, angles], -1)[:, None, :]
    return (jnp.cos(angles), jnp.sin(angles))


def turn(values, cosine, sine):
    half = ROT // 2
    part = values[..., :ROT]
    swapped = jnp.concatenate([-part[..., half:], part[..., :half]], -1)
    return jnp.concatenate([part * cosine + swapped * sine, values[..., ROT:]], -1)


def turn_back(grad, cosine, sine):
    half = ROT // 2
    part = grad[..., :ROT]
    times_sine = part * sine
    back = jnp.concatenate([times_sine[..., half:], -times_sine[..., :half]], -1)
    return jnp.concatenate([part * cosine + back, grad[..., ROT:]], -1)


def contract_rows(left, right):
    return lax.dot_general(
        left, right, (((0,), (0,)), ((), ())), preferred_element_type=jnp.float32
    )


def contract_cols(left, right):
    return lax.dot_general(
        left, right, (((1,), (1,)), ((), ())), preferred_element_type=jnp.float32
    )


def attention_scores(query, keys_all, allowed):
    scores = jnp.einsum(
        "blhd,bkhd->bhlk", query, keys_all, preferred_element_type=jnp.float32
    ) * HEAD_DIM ** (-0.5)
    return jnp.where(allowed, scores, -1e30)


def shards(
    inputs,
    cotangent,
    ln1_gain,
    ln1_bias,
    qkv_weight,
    qkv_bias,
    out_weight,
    ln2_gain,
    ln2_bias,
    gate_weight,
    up_weight,
    down_weight,
):
    batch, length, width = inputs.shape
    rows = batch * length
    scale = HEAD_DIM ** (-0.5)
    total_len = length * lax.axis_size("shard")
    first = lax.axis_index("shard") * length
    cosine, sine = rotary_tables(first, length)
    allowed = jnp.arange(total_len)[None, :] <= (first + jnp.arange(length))[:, None]
    resid_in = inputs.reshape(rows, width).astype(jnp.float32)
    gain_one, shift_one, w_qkv, bias_qkv, w_out = (
        lax.all_gather(ln1_gain, "shard", axis=0, tiled=True),
        lax.all_gather(ln1_bias, "shard", axis=0, tiled=True),
        lax.all_gather(qkv_weight, "shard", axis=0, tiled=True),
        lax.all_gather(qkv_bias, "shard", axis=0, tiled=True),
        lax.all_gather(out_weight, "shard", axis=0, tiled=True),
    )
    normed_one, scaled_one, inverse_one = normalize(resid_in, gain_one, shift_one)
    input_one = normed_one.astype(jnp.bfloat16)
    projected = jnp.dot(input_one, w_qkv, preferred_element_type=jnp.float32) + bias_qkv.astype(
        jnp.float32
    )
    projected = projected.reshape(batch, length, 3, HEADS, HEAD_DIM)
    query = turn(projected[:, :, 0], cosine, sine).astype(jnp.bfloat16)
    key_low = turn(projected[:, :, 1], cosine, sine).astype(jnp.bfloat16)
    value_low = projected[:, :, 2].astype(jnp.bfloat16)
    keys_all, values_all = (
        lax.all_gather(key_low.reshape(batch, length, width), "shard", axis=1, tiled=True),
        lax.all_gather(value_low.reshape(batch, length, width), "shard", axis=1, tiled=True),
    )
    keys_all = keys_all.reshape(batch, total_len, HEADS, HEAD_DIM)
    values_all = values_all.reshape(batch, total_len, HEADS, HEAD_DIM)
    scores = attention_scores(query, keys_all, allowed)
    top = jnp.max(scores, -1, keepdims=True)
    expo = jnp.where(allowed, jnp.exp(scores - top), 0.0)
    denom = jnp.sum(expo, -1, keepdims=True)
    log_total = top + jnp.log(denom)
    probs_low = (expo / denom).astype(jnp.bfloat16)
    mixed = jnp.einsum("bhlk,bkhd->blhd", probs_low, values_all, preferred_element_type=jnp.float32)
    attended = mixed.reshape(rows, width).astype(jnp.bfloat16)
    resid_mid = resid_in + jnp.dot(attended, w_out, preferred_element_type=jnp.float32)
    gain_two, shift_two, w_gate, w_up, w_down = (
        lax.all_gather(ln2_gain, "shard", axis=0, tiled=True),
        lax.all_gather(ln2_bias, "shard", axis=0, tiled=True),
        lax.all_gather(gate_weight, "shard", axis=0, tiled=True),
        lax.all_gather(up_weight, "shard", axis=0, tiled=True),
        lax.all_gather(down_weight, "shard", axis=0, tiled=True),
    )
    normed_two, scaled_two, inverse_two = normalize(resid_mid, gain_two, shift_two)
    input_two = normed_two.astype(jnp.bfloat16)
    gate_pre = jnp.dot(input_two, w_gate, preferred_element_type=jnp.float32)
    up_pre = jnp.dot(input_two, w_up, preferred_element_type=jnp.float32)
    sigma = jax.nn.sigmoid(gate_pre)
    silu_gate = gate_pre * sigma
    hidden = (silu_gate * up_pre).astype(jnp.bfloat16)
    resid_out = resid_mid + jnp.dot(hidden, w_down, preferred_element_type=jnp.float32)
    activations = resid_out.astype(jnp.bfloat16).reshape(batch, length, width)
    grad_out = cotangent.reshape(rows, width)
    gain_two, shift_two, w_gate, w_up, w_down = (
        lax.all_gather(ln2_gain, "shard", axis=0, tiled=True),
        lax.all_gather(ln2_bias, "shard", axis=0, tiled=True),
        lax.all_gather(gate_weight, "shard", axis=0, tiled=True),
        lax.all_gather(up_weight, "shard", axis=0, tiled=True),
        lax.all_gather(down_weight, "shard", axis=0, tiled=True),
    )
    grad_hidden = contract_cols(grad_out, w_down)
    grad_gate = (grad_hidden * up_pre * sigma * (1.0 + gate_pre * (1.0 - sigma))).astype(
        jnp.bfloat16
    )
    grad_up = (grad_hidden * silu_gate).astype(jnp.bfloat16)
    grad_normed_two = contract_cols(grad_gate, w_gate) + contract_cols(grad_up, w_up)
    gain_two_grad = jnp.sum(grad_normed_two * scaled_two, 0)
    shift_two_grad = jnp.sum(grad_normed_two, 0)
    grad_mid = grad_out.astype(jnp.float32) + normalize_back(
        grad_normed_two, gain_two, scaled_two, inverse_two
    )
    both_grads = jnp.concatenate([grad_gate, grad_up], 1)
    gate_up_grad = lax.psum_scatter(
        contract_rows(input_two, both_grads).astype(jnp.bfloat16),
        "shard",
        scatter_dimension=0,
        tiled=True,
    ).astype(jnp.float32)
    down_grad = lax.psum_scatter(
        contract_rows(hidden, grad_out).astype(jnp.bfloat16),
        "shard",
        scatter_dimension=0,
        tiled=True,
    ).astype(jnp.float32)
    gain_one, shift_one, w_qkv, bias_qkv, w_out = (
        lax.all_gather(ln1_gain, "shard", axis=0, tiled=True),
        lax.all_gather(ln1_bias, "shard", axis=0, tiled=True),
        lax.all_gather(qkv_weight, "shard", axis=0, tiled=True),
        lax.all_gather(qkv_bias, "shard", axis=0, tiled=True),
        lax.all_gather(out_weight, "shard", axis=0, tiled=True),
    )
    grad_low = grad_mid.astype(jnp.bfloat16)
    grad_mixed = (
        contract_cols(grad_low, w_out).astype(jnp.bfloat16).reshape(batch, length, HEADS, HEAD_DIM)
    )
    scores = attention_scores(query, keys_all, allowed)
    probs = jnp.where(allowed, jnp.exp(scores - log_total), 0.0)
    grad_probs = jnp.einsum(
        "blhd,bkhd->bhlk", grad_mixed, values_all, preferred_element_type=jnp.float32
    )
    row_total = jnp.sum(grad_probs * probs, -1, keepdims=True)
    grad_scores = (probs * (grad_probs - row_total)).astype(jnp.bfloat16)
    grad_query = (
        jnp.einsum("bhlk,bkhd->blhd", grad_scores, keys_all, preferred_element_type=jnp.float32)
        * scale
    )
    blocks = lax.axis_size("shard") * rows // rows
    key_part = (
        jnp.einsum("bhlk,blhd->bkhd", grad_scores, query, preferred_element_type=jnp.float32)
        * scale
    )
    value_part = jnp.einsum(
        "bhlk,blhd->bkhd", probs_low, grad_mixed, preferred_element_type=jnp.float32
    )
    joined = jnp.concatenate(
        [
            key_part.reshape(batch, blocks, length, width),
            value_part.reshape(batch, blocks, length, width),
        ],
        -1,
    )
    key_value_grad = lax.psum_scatter(
        joined.transpose(1, 0, 2, 3).reshape(blocks * rows, 2 * width).astype(jnp.bfloat16),
        "shard",
        scatter_dimension=0,
        tiled=True,
    ).astype(jnp.float32)
    grad_key = key_value_grad[:, :width].reshape(batch, length, HEADS, HEAD_DIM)
    grad_value = key_value_grad[:, width:]
    grad_qkv = jnp.concatenate(
        [
            turn_back(grad_query, cosine, sine).reshape(rows, width),
            turn_back(grad_key, cosine, sine).reshape(rows, width),
            grad_value,
        ],
        1,
    ).astype(jnp.bfloat16)
    grad_normed_one = contract_cols(grad_qkv, w_qkv)
    gain_one_grad = jnp.sum(grad_normed_one * scaled_one, 0)
    shift_one_grad = jnp.sum(grad_normed_one, 0)
    bias_qkv_grad = jnp.sum(grad_qkv, 0, dtype=jnp.float32)
    input_grad = (
        grad_mid + normalize_back(grad_normed_one, gain_one, scaled_one, inverse_one)
    ).reshape(batch, length, width)
    qkv_grad = lax.psum_scatter(
        contract_rows(input_one, grad_qkv).astype(jnp.bfloat16),
        "shard",
        scatter_dimension=0,
        tiled=True,
    ).astype(jnp.float32)
    out_grad = lax.psum_scatter(
        contract_rows(attended, grad_low).astype(jnp.bfloat16),
        "shard",
        scatter_dimension=0,
        tiled=True,
    ).astype(jnp.float32)
    gain_one_grad, shift_one_grad, bias_qkv_grad, gain_two_grad, shift_two_grad = (
        lax.psum_scatter(
            gain_one_grad.astype(jnp.bfloat16), "shard", scatter_dimension=0, tiled=True
        ).astype(jnp.float32),
        lax.psum_scatter(
            shift_one_grad.astype(jnp.bfloat16), "shard", scatter_dimension=0, tiled=True
        ).astype(jnp.float32),
        lax.psum_scatter(
            bias_qkv_grad.astype(jnp.bfloat16), "shard", scatter_dimension=0, tiled=True
        ).astype(jnp.float32),
        lax.psum_scatter(
            gain_two_grad.astype(jnp.bfloat16), "shard", scatter_dimension=0, tiled=True
        ).astype(jnp.float32),
        lax.psum_scatter(
            shift_two_grad.astype(jnp.bfloat16), "shard", scatter_dimension=0, tiled=True
        ).astype(jnp.float32),
    )
    (
        qkv_grad,
        out_grad,
        gate_up_grad,
        down_grad,
        gain_one_grad,
        shift_one_grad,
        bias_qkv_grad,
        gain_two_grad,
        shift_two_grad,
    ) = (
        lax.psum(qkv_grad.astype(jnp.bfloat16), "rep").astype(jnp.float32),
        lax.psum(out_grad.astype(jnp.bfloat16), "rep").astype(jnp.float32),
        lax.psum(gate_up_grad.astype(jnp.bfloat16), "rep").astype(jnp.float32),
        lax.psum(down_grad.astype(jnp.bfloat16), "rep").astype(jnp.float32),
        lax.psum(gain_one_grad.astype(jnp.bfloat16), "rep").astype(jnp.float32),
        lax.psum(shift_one_grad.astype(jnp.bfloat16), "rep").astype(jnp.float32),
        lax.psum(bias_qkv_grad.astype(jnp.bfloat16), "rep").astype(jnp.float32),
        lax.psum(gain_two_grad.astype(jnp.bfloat16), "rep").astype(jnp.float32),
        lax.psum(shift_two_grad.astype(jnp.bfloat16), "rep").astype(jnp.float32),
    )
    hidden_cols = gate_up_grad.shape[1] // 2
    return (
        activations,
        input_grad,
        gain_one_grad,
        shift_one_grad,
        qkv_grad,
        bias_qkv_grad,
        out_grad,
        gain_two_grad,
        shift_two_grad,
        gate_up_grad[:, :hidden_cols],
        gate_up_grad[:, hidden_cols:],
        down_grad,
    )


def solution(mesh):
    placed = (
        P("rep", "shard", None),
        P("rep", "shard", None),
        P("shard"),
        P("shard"),
        P("shard", None),
        P("shard"),
        P("shard", None),
        P("shard"),
        P("shard"),
        P("shard", None),
        P("shard", None),
        P("shard", None),
    )
    return jax.shard_map(
        shards,
        mesh=mesh,
        in_specs=placed,
        out_specs=(
            P("rep", "shard", None),
            P("rep", "shard", None),
            P("shard"),
            P("shard"),
            P("shard", None),
            P("shard"),
            P("shard", None),
            P("shard"),
            P("shard"),
            P("shard", None),
            P("shard", None),
            P("shard", None),
        ),
        check_vma=False,
    )
```

profile of v0, /device:TPU:3, one launch (start us, length us, event | category | flops | bytes accessed | tf_op | source)
XLA Modules:
  0.0 2755.8 jit_solution(17591571110782566229)
XLA Ops:
  10.0 19.9 all-gather.1
  29.9 14.6 all-gather
  44.6 27.7 %all-gather.2 = bf16[8,1,768]{2,1,0:T(2,128)(2,1)S(1)} all-gather(bf16[1,1,768]{2,1,0:T(2,128)(2,1)S(1)} %reshape.392), channel_id=1, replica_groups=mesh['shard'=8,'rep'=16] {'shard'}, dimensions={0}, use_global_device_ids=true | all-gather | bytes 13824 | tf_op jit(solution)/shard_map/all_gather | solution.py:99
  75.0 195.3 %all-gather.13.cloned.1.call-done = bf16[2048,6144]{1,0:T(8,128)(2,1)} async-done(((bf16[256,6144]{1,0:T(8,128)(2,1)}), bf16[2048,6144]{1,0:T(8,128)(2,1)}) %all-gather.13.cloned.1.call-update) | async-done | bytes 25165840 | tf_op jit(solution)/shard_map/all_gather | solution.py:98
  270.3 10.3 convolution_add_fusion
  290.6 16.0 all-gather.4
  306.6 15.5 all-gather.3
  322.4 35.2 %all-gather.17.cloned.1.call-done = bf16[1,1024,2048]{1,2,0:T(8,128)(2,1)} async-done(((bf16[1,128,2048]{1,2,0:T(8,128)(2,1)}), bf16[1,1024,2048]{1,2,0:T(8,128)(2,1)}) %all-gather.17.cloned.1.call-update) | async-done | bytes 4194320 | tf_op jit(solution)/shard_map/all_gather | solution.py:112
  357.6 4.9 fusion.52
  362.5 4.3 fusion
  368.3 5.5 divide_convert_fusion
  373.8 58.3 %all-gather.15.cloned.1.call-done = bf16[1,1024,2048]{1,2,0:T(8,128)(2,1)} async-done(((bf16[1,128,2048]{1,2,0:T(8,128)(2,1)}), bf16[1,1024,2048]{1,2,0:T(8,128)(2,1)}) %all-gather.15.cloned.1.call-update) | async-done | bytes 4194320 | tf_op jit(solution)/shard_map/all_gather | solution.py:113
  432.1 7.7 convolution_convert_fusion.6
  439.8 99.6 %all-gather.19.cloned.1.call-done = bf16[2048,2048]{1,0:T(8,128)(2,1)} async-done(((bf16[256,2048]{1,0:T(8,128)(2,1)}), bf16[2048,2048]{1,0:T(8,128)(2,1)}) %all-gather.19.cloned.1.call-update) | async-done | bytes 8388624 | tf_op jit(solution)/shard_map/all_gather | solution.py:100
  539.4 4.7 fusion.53
  545.0 234.0 %all-gather.23.cloned.1.call-done = bf16[2048,5632]{1,0:T(8,128)(2,1)} async-done(((bf16[256,5632]{1,0:T(8,128)(2,1)}), bf16[2048,5632]{1,0:T(8,128)(2,1)}) %all-gather.23.cloned.1.call-update) | async-done | bytes 23068688 | tf_op jit(solution)/shard_map/all_gather | solution.py:130
  779.0 12.6 fusion.54
  791.6 227.1 %all-gather.21.cloned.1.call-done = bf16[2048,5632]{1,0:T(8,128)(2,1)} async-done(((bf16[256,5632]{1,0:T(8,128)(2,1)}), bf16[2048,5632]{1,0:T(8,128)(2,1)}) %all-gather.21.cloned.1.call-update) | async-done | bytes 23068688 | tf_op jit(solution)/shard_map/all_gather | solution.py:129
  1018.7 12.5 fusion.55
  1031.2 227.3 %all-gather.25.cloned.1.call-done = bf16[5632,2048]{1,0:T(8,128)(2,1)} async-done(((bf16[704,2048]{1,0:T(8,128)(2,1)}), bf16[5632,2048]{1,0:T(8,128)(2,1)}) %all-gather.25.cloned.1.call-update) | async-done | bytes 23068688 | tf_op jit(solution)/shard_map/all_gather | solution.py:131
  1258.5 15.4 multiply_convert_fusion.2
  1273.9 13.4 fusion.56
  1287.3 14.3 multiply_reduce_fusion.1
  1303.5 7.1 convolution_convert_fusion.5
  1312.6 7.0 convolution_convert_fusion.4
  1319.6 12.5 multiply_reduce_fusion
  1332.1 13.0 multiply_convert_fusion
  1345.2 3.8 multiply_convert_fusion.1
  1349.7 7.7 pad_maximum_fusion
  1357.3 11.9 copy.33
  1369.3 5.6 convolution_convert_fusion.3
  1375.9 12.6 convolution_convert_fusion.1
  1388.6 7.7 fusion.7
  1397.3 84.2 %reduce-scatter.16.cloned.1.call-done = bf16[128,4096]{1,0:T(8,128)(2,1)} async-done(((bf16[1024,4096]{1,0:T(8,128)(2,1)}), bf16[128,4096]{1,0:T(8,128)(2,1)}) %reduce-scatter.16.cloned.1.call-update) | async-done | bytes 1048592
  1492.2 13.2 convolution_convert_fusion.2
  1506.1 20.9 convolution_convert_fusion
  1527.1 71.0 %reduce-scatter.12.cloned.1.call-done = bf16[256,2048]{1,0:T(8,128)(2,1)} async-done(((bf16[2048,2048]{1,0:T(8,128)(2,1)}), bf16[256,2048]{1,0:T(8,128)(2,1)}) %reduce-scatter.12.cloned.1.call-update) | async-done | bytes 1048592 | tf_op jit(solution)/shard_map/reduce_scatter | solution.py:240
  1598.1 244.9 %reduce-scatter.14.cloned.1.call-done = bf16[704,2048]{1,0:T(8,128)(2,1)} async-done(((bf16[5632,2048]{1,0:T(8,128)(2,1)}), bf16[704,2048]{1,0:T(8,128)(2,1)}) %reduce-scatter.14.cloned.1.call-update) | async-done | bytes 2883600 | tf_op jit(solution)/shard_map/reduce_scatter | solution.py:168
  1843.0 267.7 %reduce-scatter.10.cloned.1.call-done = bf16[256,6144]{1,0:T(8,128)(2,1)} async-done(((bf16[2048,6144]{1,0:T(8,128)(2,1)}), bf16[256,6144]{1,0:T(8,128)(2,1)}) %reduce-scatter.10.cloned.1.call-update) | async-done | bytes 3145744 | tf_op jit(solution)/shard_map/reduce_scatter | solution.py:234
  2110.7 453.0 %reduce-scatter.18.cloned.1.call-done = bf16[256,11264]{1,0:T(8,128)(2,1)} async-done(((bf16[2048,11264]{1,0:T(8,128)(2,1)}), bf16[256,11264]{1,0:T(8,128)(2,1)}) %reduce-scatter.18.cloned.1.call-update) | async-done | bytes 5767184
  2566.4 12.0 fusion.6
  2578.9 13.8 fusion.22
  2592.8 34.5 %all-reduce.8 = (bf16[2048]{0:T(1024)(128)(2,1)S(1)}, bf16[2048]{0:T(1024)(128)(2,1)S(1)}, bf16[6144]{0:T(1024)(128)(2,1)S(1)}, bf16[2048]{0:T(1024)(128)(2,1)S(1)}, bf16[2048]{0:T(1024)(128)(2,1)S(1)}) all-reduce(bf16[2048]{0:T(1024)(128)(2,1)S(1)} %get-tuple-element.14, ...), channel_id=3, replica_groups=mesh['shard'=8,'rep'=16] {'shard'}, use_global_device_ids=true, to_apply=%region_13.14.clone | all-reduce | flops 14336 | bytes 57344
  2627.7 36.4 %all-reduce.6 = (bf16[256]{0:T(256)(128)(2,1)S(1)}, bf16[256]{0:T(256)(128)(2,1)S(1)}, bf16[768]{0:T(1024)(128)(2,1)S(1)}, bf16[256]{0:T(256)(128)(2,1)S(1)}, bf16[256]{0:T(256)(128)(2,1)S(1)}) all-reduce(bf16[256]{0:T(256)(128)(2,1)S(1)} %dynamic-slice.1, ...), channel_id=1, replica_groups=mesh['shard'=8,'rep'=16] {'rep'}, use_global_device_ids=true, to_apply=%region_14.15 | all-reduce | flops 1792 | bytes 7168 | tf_op jit(solution)/shard_map/psum | solution.py:278
  2668.4 62.7 %all-reduce.11.cloned.1.call-done = (bf16[256,6144]{1,0:T(8,128)(2,1)}, bf16[256,2048]{1,0:T(8,128)(2,1)}, bf16[256,11264]{1,0:T(8,128)(2,1)}, bf16[704,2048]{1,0:T(8,128)(2,1)}) async-done(((bf16[256,6144]{1,0:T(8,128)(2,1)}, bf16[256,2048]{1,0:T(8,128)(2,1)}, bf16[256,11264]{1,0:T(8,128)(2,1)}, bf16[704,2048]{1,0:T(8,128)(2,1)}), (bf16[256,6144]{1,0:T(8,128)(2,1)}, bf16[256,2048]{1,0:T(8,128)(2,1)}, ...) | async-done | bytes 12845072 | tf_op jit(solution)/shard_map/psum | solution.py:274
  2734.1 5.5 convert_element_type.220
  2739.6 3.3 convert_element_type.231
  2742.9 5.9 fusion.48
  (174 shorter events, 45.4 us)
Async XLA Ops:
  7.2 263.2 %all-gather.13.cloned.1.call-start = ((), (), s32[]{:S(2)}) async-start(), calls=%async_computation.5 | async-start | bytes 28311552 | tf_op jit(solution)/shard_map/all_gather | solution.py:98
  7.9 349.7 %all-gather.17.cloned.1.call-start = ((), (), s32[]{:S(2)}) async-start(), calls=%async_computation.7 | async-start | bytes 4718592 | tf_op jit(solution)/shard_map/all_gather | solution.py:112
  29.9 250.7 %copy-start.21 = (f32[8,1,256]{2,1,0:T(1,128)}, f32[8,1,256]{2,1,0:T(1,128)S(1)}, u32[]{:S(2)}) copy-start(f32[8,1,256]{2,1,0:T(1,128)S(1)} %convert_element_type.233) | copy-start | bytes 24580
  44.6 236.0 %copy-start.19 = (f32[8,1,256]{2,1,0:T(1,128)}, f32[8,1,256]{2,1,0:T(1,128)S(1)}, u32[]{:S(2)}) copy-start(f32[8,1,256]{2,1,0:T(1,128)S(1)} %convert_element_type.232) | copy-start | bytes 24580
  72.4 212.4 %copy-start.29 = (f32[128,16]{0,1:T(8,128)}, f32[128,16]{0,1:T(8,128)S(1)}, u32[]{:S(2)}) copy-start(f32[128,16]{0,1:T(8,128)S(1)} %get-tuple-element.57) | copy-start | bytes 24580
  72.4 212.4 %copy-start.30 = (f32[128,16]{0,1:T(8,128)}, f32[128,16]{0,1:T(8,128)S(1)}, u32[]{:S(2)}) copy-start(f32[128,16]{0,1:T(8,128)S(1)} %get-tuple-element.58) | copy-start | bytes 24580
  73.6 207.0 %copy-start.31 = (f32[128]{0:T(128)}, f32[128]{0:T(128)S(1)}, u32[]{:S(2)}) copy-start(f32[128]{0:T(128)S(1)} %broadcast_multiply_fusion.6) | copy-start | bytes 1540
  75.0 205.6 %copy-start.33 = (f32[128]{0:T(128)}, f32[128]{0:T(128)S(1)}, u32[]{:S(2)}) copy-start(f32[128]{0:T(128)S(1)} %add_rsqrt_fusion.1) | copy-start | bytes 1540
  284.9 72.7 %copy-start.17 = (bf16[128,32,16]{0,2,1:T(8,128)(2,1)}, bf16[128,32,16]{0,2,1:T(8,128)(2,1)S(1)}, u32[]{:S(2)}) copy-start(bf16[128,32,16]{0,2,1:T(8,128)(2,1)S(1)} %get-tuple-element.51) | copy-start | bytes 393220
  285.8 4.7 copy-start.37
  285.8 4.8 copy-start.38
  285.8 146.2 %all-gather.15.cloned.1.call-start = ((), (), s32[]{:S(2)}) async-start(), calls=%async_computation.6 | async-start | bytes 4718592 | tf_op jit(solution)/shard_map/all_gather | solution.py:113
  288.0 251.4 %all-gather.19.cloned.1.call-start = ((), (), s32[]{:S(2)}) async-start(), calls=%async_computation.8 | async-start | bytes 9437184 | tf_op jit(solution)/shard_map/all_gather | solution.py:100
  288.6 490.4 %all-gather.23.cloned.1.call-start = ((), (), s32[]{:S(2)}) async-start(), calls=%async_computation.10 | async-start | bytes 25952256 | tf_op jit(solution)/shard_map/all_gather | solution.py:130
  289.2 729.5 %all-gather.21.cloned.1.call-start = ((), (), s32[]{:S(2)}) async-start(), calls=%async_computation.9 | async-start | bytes 25952256 | tf_op jit(solution)/shard_map/all_gather | solution.py:129
  289.8 968.7 %all-gather.25.cloned.1.call-start = ((), (), s32[]{:S(2)}) async-start(), calls=%async_computation.11 | async-start | bytes 25952256 | tf_op jit(solution)/shard_map/all_gather | solution.py:131
  290.5 1191.0 %reduce-scatter.16.cloned.1.call-start = ((), (), s32[]{:S(2)}) async-start(), calls=%async_computation.15 | async-start | bytes 9437184
  322.3 44.5 %copy-start.6 = (pred[128,1024]{1,0:T(8,128)(4,1)}, pred[128,1024]{1,0:T(8,128)(4,1)S(1)}, u32[]{:S(2)}) copy-start(pred[128,1024]{1,0:T(8,128)(4,1)S(1)} %iota_compare_fusion) | copy-start | bytes 393220
  322.4 40.1 %copy-start.12 = (bf16[128,32,48]{0,2,1:T(8,128)(2,1)}, bf16[128,32,48]{0,2,1:T(8,128)(2,1)S(1)}, u32[]{:S(2)}) copy-start(bf16[128,32,48]{0,2,1:T(8,128)(2,1)S(1)} %fusion.27) | copy-start | bytes 1179652
  362.5 5.8 copy-start
  432.1 107.3 %copy-start.2 = (bf16[1,128,2048]{2,1,0:T(8,128)(2,1)S(1)}, bf16[1,128,2048]{2,1,0:T(8,128)(2,1)}, u32[]{:S(2)}) copy-start(bf16[1,128,2048]{2,1,0:T(8,128)(2,1)} %param.12) | copy-start | bytes 1572868
  544.1 474.6 %copy-start.23 = (f32[128]{0:T(128)}, f32[128]{0:T(128)S(1)}, u32[]{:S(2)}) copy-start(f32[128]{0:T(128)S(1)} %broadcast_multiply_fusion.5) | copy-start | bytes 1540
  544.4 474.3 %copy-start.26 = (f32[128]{0:T(128)}, f32[128]{0:T(128)S(1)}, u32[]{:S(2)}) copy-start(f32[128]{0:T(128)S(1)} %add_rsqrt_fusion) | copy-start | bytes 1540
  1273.9 13.4 copy-start.4
  1273.9 13.4 copy-start.5
  1273.9 13.4 copy-start.24
  1273.9 13.4 copy-start.27
  1312.6 7.0 copy-start.3
  1312.6 7.0 copy-start.7
  1312.6 7.0 copy-start.10
  1312.6 7.0 copy-start.22
  1332.1 13.0 copy-start.13
  1332.1 13.1 copy-start.18
  1369.3 228.8 %reduce-scatter.12.cloned.1.call-start = ((), (), s32[]{:S(2)}) async-start(), calls=%async_computation.13 | async-start | bytes 9437184 | tf_op jit(solution)/shard_map/reduce_scatter | solution.py:240
  1374.9 468.1 %reduce-scatter.14.cloned.1.call-start = ((), (), s32[]{:S(2)}) async-start(), calls=%async_computation.14 | async-start | bytes 25952256 | tf_op jit(solution)/shard_map/reduce_scatter | solution.py:168
  1388.5 722.2 %reduce-scatter.10.cloned.1.call-start = ((), (), s32[]{:S(2)}) async-start(), calls=%async_computation.12 | async-start | bytes 28311552 | tf_op jit(solution)/shard_map/reduce_scatter | solution.py:234
  1505.5 1058.3 %reduce-scatter.18.cloned.1.call-start = ((), (), s32[]{:S(2)}) async-start(), calls=%async_computation.16 | async-start | bytes 51904512
  1527.0 1204.1 %all-reduce.11.cloned.1.call-start = ((), (), s32[]{:S(2)}) async-start(), calls=%async_computation.17 | async-start | bytes 25690112 | tf_op jit(solution)/shard_map/psum | solution.py:274
  2566.3 12.1 copy-start.8
  2566.3 12.1 copy-start.9
  2566.3 12.6 copy-start.20
  2566.3 12.6 copy-start.32
  2566.4 12.6 copy-start.34
  2578.9 13.8 copy-start.35
  2578.9 13.8 copy-start.36
  2731.1 8.4 copy-start.14
  2734.1 8.8 slice-start
  2734.1 8.8 slice-start.1
  (7 other events, 9.4 us)
Sparse Core Ops, SparseCore 0:
  10.3 259.9 all-gather.12
  285.9 71.6 all-gather.16
  360.4 71.6 all-gather.14
  434.3 105.0 all-gather.18
  541.5 237.4 all-gather.22
  781.2 237.4 all-gather.20
  1021.0 237.4 all-gather.24
  1369.4 112.0 reduce-scatter.15
  1485.8 112.2 reduce-scatter.11
  1601.9 241.0 reduce-scatter.13
  1847.0 263.6 reduce-scatter.9
  2114.6 449.1 reduce-scatter.17
  2566.8 164.2 all-reduce.10
where the time goes:
time: 2760 us
  waiting for transfers between devices  2260 us (82%)
  matrix products  212 us (8%)
  blocking collectives  165 us (6%)
  other arithmetic  58.5 us (2%)
  local copies, waits for them, and re-layouts  40.4 us (1%)
    unnamed x15, waiting for transfers between devices  540 us
    reduce_scatter x1, waiting for transfers between devices, shards(): lax.psum_scatter(contract_rows(input_one, grad_qkv).astype(jnp.bfloat16),...  268 us
    reduce_scatter x1, waiting for transfers between devices, shards(): lax.psum_scatter(contract_rows(hidden, grad_out).astype(jnp.bfloat16), 's...  245 us
    all_gather x1, waiting for transfers between devices, shards(): lax.all_gather(up_weight, 'shard', axis=0, tiled=True)  234 us
    all_gather x1, waiting for transfers between devices, shards(): lax.all_gather(down_weight, 'shard', axis=0, tiled=True)  227 us
    all_gather x1, waiting for transfers between devices, shards(): lax.all_gather(gate_weight, 'shard', axis=0, tiled=True)  227 us
    all_gather x1, waiting for transfers between devices, shards(): lax.all_gather(qkv_weight, 'shard', axis=0, tiled=True)  195 us
    all_gather x1, waiting for transfers between devices, shards(): lax.all_gather(out_weight, 'shard', axis=0, tiled=True)  99.6 us
  transfers between devices with their start and end apart: 13, of which 13 were waited for; matrix products, arithmetic and copies ran while one was open for 6% of the time, Pallas kernels for 0%

commit v1 on v0

v1 whole, which is shorter than its diff:
```python
import functools

import jax
import jax.numpy as jnp
import numpy as np
from jax import lax
from jax.experimental import pallas as pl
from jax.experimental.pallas import tpu as pltpu
from jax.sharding import PartitionSpec as P

HEADS = 32
HEAD_DIM = 64
ROT = 16
WIDTH = 2048
GROUP = 8
REPS = 16
ROWS = 128
TOTAL = GROUP * ROWS
LOCAL = WIDTH // GROUP
LOCAL_HEADS = HEADS // GROUP
FF = 5632
LOCAL_FF = FF // GROUP
HID = 768
SLAB = LOCAL // REPS
CHUNK = 256
CHUNKS = TOTAL // CHUNK
EPS = 1e-05
BASE = 10000.0
BF = jnp.bfloat16
F32 = jnp.float32
MESH = pl.DeviceIdType.MESH
VM = pl.BlockSpec(memory_space=pltpu.VMEM)
ANY = pl.BlockSpec(memory_space=pl.ANY)
DMA = pltpu.SemaphoreType.DMA


def dot(left, right):
    return jnp.dot(left, right, preferred_element_type=F32)


def dot_nt(left, right):
    return lax.dot_general(left, right, (((1,), (1,)), ((), ())), preferred_element_type=F32)


FAR, UP, DOWN = (1, 0, 0, 0, 0), (0, 1, 0, 0, 0), (0, -1, 0, 0, 0)
NEAR, NORTH, SOUTH, TWIN = (0, 0, 1, 0, 0), (0, 0, 0, 1, 0), (0, 0, 0, -1, 0), (0, 0, 0, 0, 1)
HERE = (0, 0, 0, 0, 0)
SIZES = (2, 4, 2, 4, 2)
PEERS = tuple((f, z, 0, 0, 0) for f in range(2) for z in range(4) if (f, z) != (0, 0))


def place():
    shard, rep = lax.axis_index("shard"), lax.axis_index("rep")
    return (shard // 4, lax.rem(shard, 4), rep // 8, lax.rem(rep // 2, 4), lax.rem(rep, 2))


def shift(where, offset):
    return tuple(
        lax.rem(a + (o + 2 * n) % n, n) if o % n else a for a, o, n in zip(where, offset, SIZES)
    )


def shard_at(where, offset=HERE):
    far, level = shift(where, offset)[:2]
    return far * 4 + level


def rep_at(where, offset=HERE):
    near, north, core = shift(where, offset)[2:]
    return near * 8 + north * 2 + core


def device(where, offset):
    return (shard_at(where, offset), rep_at(where, offset))


def less(a, b):
    return tuple((p - q) % n for p, q, n in zip(a, b, SIZES))


def negative(a):
    return tuple(-p for p in a)


def greet(where, offsets):
    barrier = pltpu.get_barrier_semaphore()
    for offset in offsets:
        pl.semaphore_signal(
            barrier, inc=1, device_id=device(where, negative(offset)), device_id_type=MESH
        )
    pl.semaphore_wait(barrier, len(offsets))


def remote(src, dst, sends, recvs, i, to):
    return pltpu.make_async_remote_copy(
        src_ref=src,
        dst_ref=dst,
        send_sem=sends.at[i],
        recv_sem=recvs.at[i],
        device_id=to,
        device_id_type=MESH,
    )


def token_moves():
    moves = []

    def add(owner, part, step, first, turn):
        moves.append((owner, part, step, first, turn))
        return len(moves) - 1

    near, far = (0, WIDTH // 2), (WIDTH // 2, WIDTH // 2)
    whole, top, low = (0, ROWS), (0, ROWS // 2), (ROWS // 2, ROWS // 2)
    up2 = (0, 2, 0, 0, 0)
    up = add(HERE, (whole, near), UP, None, 0)
    down = add(HERE, (whole, near), DOWN, None, 0)
    add(HERE, (whole, near), FAR, None, 0.2)
    a = add(DOWN, (top, near), UP, up, 1)
    b = add(UP, (low, near), DOWN, down, 1)
    add(DOWN, (whole, near), FAR, up, 1.1)
    add(UP, (whole, near), FAR, down, 1.1)
    add(up2, (top, near), FAR, a, 2)
    add(up2, (low, near), FAR, b, 2)
    over = add(HERE, (whole, far), FAR, None, 1)
    up = add(HERE, (whole, far), UP, None, 1.1)
    down = add(HERE, (whole, far), DOWN, None, 1.1)
    add(DOWN, (top, far), UP, up, 3)
    add(UP, (low, far), DOWN, down, 3)
    up = add(FAR, (whole, far), UP, over, 2.5)
    down = add(FAR, (whole, far), DOWN, over, 2.5)
    add(tuple(p + q for p, q in zip(FAR, DOWN)), (top, far), UP, up, 4)
    add(tuple(p + q for p, q in zip(FAR, UP)), (low, far), DOWN, down, 4)
    return tuple(moves)


MOVES = token_moves()
COUNT = len(MOVES)
TURNS = tuple(sorted(range(COUNT), key=lambda i: MOVES[i][4]))
FED = tuple(tuple(j for j in range(COUNT) if MOVES[j][3] == i) for i in range(COUNT))
NEIGHBOURS = (FAR, UP, DOWN)
LANDS = {}
for _i in range(COUNT):
    LANDS[_i] = _i
LANDINGS = COUNT


def token_part(ref, block, part):
    (row, rows), (col, cols) = part
    return ref.at[block, pl.ds(row, rows), pl.ds(col, cols)]


class Gather:
    def __init__(self, where, ref, sends, recvs):
        self.where, self.ref, self.sends, self.recvs = where, ref, sends, recvs
        self.got = set()

    def move(self, i, arriving=False):
        owner, part, step, _, _ = MOVES[i]
        block = shard_at(self.where, less(owner, step) if arriving else owner)
        ref = token_part(self.ref, block, part)
        return remote(ref, ref, self.sends, self.recvs, i, device(self.where, step))

    def take(self, i):
        if i not in self.got:
            self.got.add(i)
            self.move(i, True).wait_recv()

    def turn(self, i):
        if MOVES[i][3] is not None:
            self.take(MOVES[i][3])
        self.move(i).start()

    def finish(self):
        for i in TURNS:
            self.take(i)
        for i in TURNS:
            self.move(i).wait_send()

    def run(self):
        for i in TURNS:
            self.turn(i)
        self.finish()


class Scatter:
    def __init__(self, where, buf, land, sends, recvs):
        self.where, self.buf, self.land, self.sends, self.recvs = where, buf, land, sends, recvs
        self.got = set()

    def move(self, i, arriving=False):
        owner, part, step, _, _ = MOVES[i]
        block = shard_at(self.where, owner if arriving else less(owner, step))
        (row, rows), (col, cols) = part
        return remote(
            token_part(self.buf, block, part),
            self.land.at[LANDS[i], pl.ds(row, rows)],
            self.sends,
            self.recvs,
            i,
            device(self.where, negative(step)),
        )

    def take(self, i):
        if i in self.got:
            return
        self.got.add(i)
        owner, ((row, rows), (col, cols)), _, _, _ = MOVES[i]
        self.move(i, True).wait_recv()
        at = (shard_at(self.where, owner), pl.ds(row, rows), pl.ds(col, cols))
        total = self.buf[at].astype(F32) + self.land[LANDS[i], pl.ds(row, rows)].astype(F32)
        self.buf[at] = total.astype(BF)

    def turn(self, i):
        for j in FED[i]:
            self.take(j)
        self.move(i).start()

    def finish(self):
        for i in reversed(TURNS):
            self.take(i)
        for i in reversed(TURNS):
            self.move(i).wait_send()

    def run(self):
        for i in reversed(TURNS):
            self.turn(i)
        self.finish()


def slab_moves():
    moves = []

    def add(owner, part, step, first, turn):
        moves.append((owner, part, step, first, turn))
        return len(moves) - 1

    whole, half, rest = (0, GROUP), (0, GROUP // 2), (GROUP // 2, GROUP // 2)
    near = add(HERE, whole, NEAR, None, 0)
    for base, first, turn in ((HERE, None, 0), (NEAR, near, 1)):
        def at(*steps):
            return tuple(sum(p) for p in zip(base, *steps))

        up = add(base, whole, NORTH, first, turn)
        down = add(base, whole, SOUTH, first, turn)
        add(base, whole, TWIN, first, turn + 0.1)
        a = add(at(SOUTH), half, NORTH, up, turn + 2)
        b = add(at(NORTH), rest, SOUTH, down, turn + 2)
        add(at(SOUTH), whole, TWIN, up, turn + 2.1)
        add(at(NORTH), whole, TWIN, down, turn + 2.1)
        add(at(NORTH, NORTH), half, TWIN, a, turn + 4)
        add(at(NORTH, NORTH), rest, TWIN, b, turn + 4)
    return tuple(moves)


SLABS = slab_moves()
SLAB_COUNT = len(SLABS)
SLAB_TURNS = tuple(sorted(range(SLAB_COUNT), key=lambda i: SLABS[i][4]))
SLAB_FED = tuple(tuple(j for j in range(SLAB_COUNT) if SLABS[j][3] == i) for i in range(SLAB_COUNT))
SLAB_LANDS = {}
for _i in range(SLAB_COUNT):
    if SLABS[_i][1][0] == 0:
        SLAB_LANDS[_i] = len(set(SLAB_LANDS.values()))
    else:
        SLAB_LANDS[_i] = SLAB_LANDS[_i - 1] if SLABS[_i - 1][1][1] < GROUP else None
SLAB_LANDINGS = len(set(SLAB_LANDS.values()))
REP_NEIGHBOURS = (NEAR, NORTH, SOUTH, TWIN)


class Spread:
    def __init__(self, where, cuts, ref, own_sem, first_sends, first_recvs, sends, recvs):
        self.where, self.cuts, self.ref, self.own_sem = where, cuts, ref, own_sem
        self.first_sends, self.first_recvs = first_sends, first_recvs
        self.slabs = SlabGather(where, ref, sends, recvs)

    def first(self, n, offset, arriving=False):
        me, rep = shard_at(self.where), rep_at(self.where)
        owner = shard_at(self.where, negative(offset)) if arriving else me
        copies = []
        for j, (src, (col, cols)) in enumerate(self.cuts(shard_at(self.where, offset))):
            copies.append(
                remote(
                    src,
                    self.ref.at[owner, rep, :, pl.ds(col, cols)],
                    self.first_sends,
                    self.first_recvs,
                    (n, j),
                    device(self.where, offset),
                )
            )
        return copies

    def own(self):
        me, rep = shard_at(self.where), rep_at(self.where)
        return [
            pltpu.make_async_copy(
                src, self.ref.at[me, rep, :, pl.ds(col, cols)], self.own_sem.at[j]
            )
            for j, (src, (col, cols)) in enumerate(self.cuts(me))
        ]

    def begin(self):
        for n, offset in enumerate(PEERS):
            for copy in self.first(n, offset):
                copy.start()
        for copy in self.own():
            copy.start()

    def middle(self):
        for copy in self.own():
            copy.wait()
        for n, offset in enumerate(PEERS):
            for copy in self.first(n, offset, True):
                copy.wait_recv()

    def finish(self):
        self.slabs.finish()
        for n, offset in enumerate(PEERS):
            for copy in self.first(n, offset):
                copy.wait_send()

    def turn(self, i):
        self.slabs.turn(i)


class SlabGather:
    def __init__(self, where, ref, sends, recvs):
        self.where, self.ref, self.sends, self.recvs = where, ref, sends, recvs
        self.got = set()

    def move(self, i, arriving=False):
        owner, (first, count), step, _, _ = SLABS[i]
        rep = rep_at(self.where, less(owner, step) if arriving else owner)
        scale = self.ref.shape[0]
        ref = self.ref.at[pl.ds(first * scale // GROUP, count * scale // GROUP), rep]
        return remote(ref, ref, self.sends, self.recvs, i, device(self.where, step))

    def take(self, i):
        if i not in self.got:
            self.got.add(i)
            self.move(i, True).wait_recv()

    def turn(self, i):
        if SLABS[i][3] is not None:
            self.take(SLABS[i][3])
        self.move(i).start()

    def finish(self):
        for i in SLAB_TURNS:
            self.take(i)
        for i in SLAB_TURNS:
            self.move(i).wait_send()


class SlabScatter:
    def __init__(self, where, ref, land, sends, recvs):
        self.where, self.ref, self.land, self.sends, self.recvs = where, ref, land, sends, recvs
        self.got = set()

    def span(self, i):
        first, count = SLABS[i][1]
        scale = self.ref.shape[0]
        return pl.ds(first * scale // GROUP, count * scale // GROUP)

    def move(self, i, arriving=False):
        owner, _, step, _, _ = SLABS[i]
        rep = rep_at(self.where, owner if arriving else less(owner, step))
        return remote(
            self.ref.at[self.span(i), rep],
            self.land.at[SLAB_LANDS[i], self.span(i)],
            self.sends,
            self.recvs,
            i,
            device(self.where, negative(step)),
        )

    def take(self, i):
        if i in self.got:
            return
        self.got.add(i)
        self.move(i, True).wait_recv()
        first, count = SLABS[i][1]
        scale = self.ref.shape[0]
        rep = rep_at(self.where, SLABS[i][0])

        @pl.loop(first * scale // GROUP, (first + count) * scale // GROUP)
        def _(n):
            total = self.ref[n, rep].astype(F32) + self.land[SLAB_LANDS[i], n].astype(F32)
            self.ref[n, rep] = total.astype(BF)

    def turn(self, i):
        for j in SLAB_FED[i]:
            self.take(j)
        self.move(i).start()

    def finish(self):
        for i in reversed(SLAB_TURNS):
            self.take(i)
        for i in reversed(SLAB_TURNS):
            self.move(i).wait_send()


def spread_scratch(cuts):
    return [DMA((cuts,)), DMA((7, cuts)), DMA((7, cuts)), DMA((SLAB_COUNT,)), DMA((SLAB_COUNT,))]


def qkv_cuts(w_ref, rep):
    rows = pl.ds(pl.multiple_of(rep * SLAB, SLAB), SLAB)

    def cuts(shard):
        return [
            (
                w_ref.at[rows, pl.ds(pl.multiple_of(j * WIDTH + shard * LOCAL, LOCAL), LOCAL)],
                (j * LOCAL, LOCAL),
            )
            for j in range(3)
        ]

    return cuts


def hidden_start(shard):
    return (shard // 2) * (2 * LOCAL_FF) + lax.rem(shard, 2) * (5 * 128)


def gate_up_cuts(gate_ref, up_ref, rep):
    rows = pl.ds(pl.multiple_of(rep * SLAB, SLAB), SLAB)

    def cuts(shard):
        cols = pl.ds(pl.multiple_of(hidden_start(shard), 128), HID)
        return [(gate_ref.at[rows, cols], (0, HID)), (up_ref.at[rows, cols], (HID, HID))]

    return cuts


def normalize(values, gain, shift_):
    center = values - jnp.mean(values, -1, keepdims=True)
    inverse = lax.rsqrt(jnp.mean(center * center, -1, keepdims=True) + EPS)
    scaled = center * inverse
    return (scaled * gain + shift_, scaled, inverse)


def normalize_back(grad, gain, scaled, inverse):
    weighted = grad * gain
    return inverse * (
        weighted
        - jnp.mean(weighted, -1, keepdims=True)
        - scaled * jnp.mean(weighted * scaled, -1, keepdims=True)
    )


def small_row(small_ref, row):
    return jnp.concatenate([small_ref[s, row : row + 1, :] for s in range(GROUP)], axis=1)


def rotary_tables():
    positions = np.arange(TOTAL, dtype=np.float32)
    freqs = np.float32(BASE) ** (-np.arange(0, ROT, 2).astype(np.float32) / np.float32(ROT))
    angles = positions[:, None] * freqs[None, :].astype(np.float32)
    cosine, sine = np.cos(angles).astype(np.float32), np.sin(angles).astype(np.float32)
    half = ROT // 2
    one = np.ones((TOTAL, HEAD_DIM), np.float32)
    low, high = np.zeros((TOTAL, HEAD_DIM), np.float32), np.zeros((TOTAL, HEAD_DIM), np.float32)
    one[:, :half], one[:, half:ROT] = cosine, cosine
    low[:, :half] = -sine
    high[:, half:ROT] = sine
    return np.stack([np.concatenate([t, t], 1) for t in (one, low, high)])


def turned(values, table_ref, rows, sign):
    parts = []
    for side in range(2):
        part = values[:, side * 128 : (side + 1) * 128]
        swing = pltpu.roll(part, 128 - ROT // 2, 1) * table_ref[1, rows, :] + (
            pltpu.roll(part, ROT // 2, 1) * table_ref[2, rows, :]
        )
        straight = part * table_ref[0, rows, :]
        parts.append(straight + swing if sign > 0 else straight - swing)
    return jnp.concatenate(parts, axis=1)


def chunk_rows(i):
    return pl.ds(pl.multiple_of(i * CHUNK, CHUNK), CHUNK)


def token_chunk(ref, i):
    return ref[pl.ds(i * 2, 2)].reshape(CHUNK, WIDTH)


def bias_row(small_ref, shard, j):
    block = j * GROUP + shard
    return small_ref[block // 3, pl.ds(4 + lax.rem(block, 3), 1), :]


def project(shard, tokens_ref, w_ref, small_ref, table_ref, q_ref, k_ref, v_ref):
    @pl.loop(0, CHUNKS)
    def _(i):
        rows = chunk_rows(i)
        tokens = token_chunk(tokens_ref, i)
        for j, ref in enumerate((q_ref, k_ref, v_ref)):
            w = w_ref[:, :, :, j * LOCAL : (j + 1) * LOCAL].reshape(WIDTH, LOCAL)
            value = dot(tokens, w) + bias_row(small_ref, shard, j)
            if j < 2:
                value = turned(value, table_ref, rows, 1)
            if j == 0:
                value = value * HEAD_DIM ** (-0.5)
            ref[rows, :] = value.astype(BF)


def head_lanes(h):
    return lax.broadcasted_iota(jnp.int32, (CHUNK, LOCAL), 1) // HEAD_DIM == h


def allowed_keys(i):
    keys = CHUNK * (i + 1)
    return lax.broadcasted_iota(jnp.int32, (keys, CHUNK), 0) <= (
        lax.broadcasted_iota(jnp.int32, (keys, CHUNK), 1) + CHUNK * i
    )


def attend(q_ref, k_ref, v_ref, vt_ref, mixed_ref, att_ref, lse_ref):
    vt_ref[...] = v_ref[...].astype(F32).T.astype(BF)
    for i in range(CHUNKS):
        keys = CHUNK * (i + 1)
        cols = slice(CHUNK * i, keys)

        @pl.loop(0, LOCAL_HEADS)
        def _(h):
            query = jnp.where(head_lanes(h), q_ref[cols, :], jnp.zeros((), BF))
            scores = dot_nt(k_ref[:keys, :], query)
            scores = jnp.where(allowed_keys(i), scores, -1e30)
            top = jnp.max(scores, 0, keepdims=True)
            expo = jnp.exp(scores - top)
            denom = jnp.sum(expo, 0, keepdims=True)
            probs_low = (expo * (1.0 / denom)).astype(BF)
            lanes = pl.ds(pl.multiple_of(h * HEAD_DIM, HEAD_DIM), HEAD_DIM)
            mixed_ref[lanes, cols] = dot(vt_ref[lanes, :keys], probs_low)
            lse_ref[pl.ds(h, 1), cols] = top + jnp.log(denom)

        att_ref[cols, :] = mixed_ref[:, cols].T.astype(BF)


def attend_back(q_ref, k_ref, v_ref, da_ref, lse_ref, kt_ref, dqt_ref, dk_ref, dv_ref):
    kt_ref[...] = k_ref[...].astype(F32).T.astype(BF)
    dk_ref[...] = jnp.zeros_like(dk_ref)
    dv_ref[...] = jnp.zeros_like(dv_ref)
    for i in range(CHUNKS):
        keys = CHUNK * (i + 1)
        cols = slice(CHUNK * i, keys)

        @pl.loop(0, LOCAL_HEADS)
        def _(h):
            query = jnp.where(head_lanes(h), q_ref[cols, :], jnp.zeros((), BF))
            grad = jnp.where(head_lanes(h), da_ref[cols, :], jnp.zeros((), BF))
            scores = dot_nt(k_ref[:keys, :], query)
            probs = jnp.where(allowed_keys(i), jnp.exp(scores - lse_ref[pl.ds(h, 1), cols]), 0.0)
            grad_probs = dot_nt(v_ref[:keys, :], grad)
            total = jnp.sum(grad_probs * probs, 0, keepdims=True)
            grad_scores = (probs * (grad_probs - total)).astype(BF)
            dv_ref[:keys, :] += dot(probs.astype(BF), grad)
            dk_ref[:keys, :] += dot(grad_scores, query)
            lanes = pl.ds(pl.multiple_of(h * HEAD_DIM, HEAD_DIM), HEAD_DIM)
            dqt_ref[lanes, cols] = dot(kt_ref[lanes, :keys], grad_scores)


def times(left_ref, w_ref, out_ref):
    @pl.loop(0, CHUNKS)
    def _(i):
        left = left_ref[chunk_rows(i), :]
        for j in range(WIDTH // 512):
            cols = slice(j * 512, (j + 1) * 512)
            out_ref[pl.ds(i * 2, 2), :, cols] = (
                dot(left, w_ref[:, cols]).astype(BF).reshape(2, ROWS, 512)
            )


def times_back(left_ref, w_ref, out_ref):
    depth = left_ref.shape[1]

    @pl.loop(0, CHUNKS)
    def _(i):
        left = left_ref[chunk_rows(i), :]
        for j in range(GROUP):
            w = w_ref[j].reshape(LOCAL, depth)
            out_ref[pl.ds(i * 2, 2), :, j * LOCAL : (j + 1) * LOCAL] = (
                dot_nt(left, w).astype(BF).reshape(2, ROWS, LOCAL)
            )


def feed_forward(shard, tokens_ref, grads_ref, w_ref, down_ref, hid_ref, dgu_ref):
    odd = lax.rem(shard, 2)

    @pl.loop(0, CHUNKS)
    def _(i):
        rows = chunk_rows(i)
        tokens, grads = token_chunk(tokens_ref, i), token_chunk(grads_ref, i)
        for j in range(HID // CHUNK):
            cols = slice(j * CHUNK, (j + 1) * CHUNK)
            late = slice(HID + j * CHUNK, HID + (j + 1) * CHUNK)
            gate = dot(tokens, w_ref[:, :, :, cols].reshape(WIDTH, CHUNK))
            up = dot(tokens, w_ref[:, :, :, late].reshape(WIDTH, CHUNK))
            grad = dot_nt(grads, down_ref[cols, :])
            unit = lax.broadcasted_iota(jnp.int32, (CHUNK, CHUNK), 1) + (j * CHUNK - 64 * odd)
            mine = jnp.logical_and(unit >= 0, unit < LOCAL_FF)
            sigma = 1.0 / (1.0 + jnp.exp(-gate))
            silu = gate * sigma
            hid_ref[rows, cols] = jnp.where(mine, silu * up, 0.0).astype(BF)
            grad_gate = grad * up * (sigma * (1.0 + gate * (1.0 - sigma)))
            dgu_ref[rows, cols] = jnp.where(mine, grad_gate, 0.0).astype(BF)
            dgu_ref[rows, late] = jnp.where(mine, grad * silu, 0.0).astype(BF)


def outer(left_ref, right_ref, out_ref):
    depth = out_ref.shape[-1]
    tiles = left_ref.shape[-1] // LOCAL

    @pl.loop(0, tiles)
    def _(m):
        cols = pl.ds(pl.multiple_of(m * LOCAL, LOCAL), LOCAL)
        if len(left_ref.shape) == 3:
            left = left_ref[:, :, cols].reshape(TOTAL, LOCAL)
        else:
            left = left_ref[:, cols]
        left = left.astype(F32).T.astype(BF)
        for j in range(depth // 512 if depth % 512 == 0 else depth // 256):
            size = 512 if depth % 512 == 0 else 256
            part = slice(j * size, (j + 1) * size)
            if len(right_ref.shape) == 3:
                right = right_ref[:, :, part].reshape(TOTAL, size)
            else:
                right = right_ref[:, part]
            out_ref[cols, part] = dot(left, right).astype(BF)


def params(cid=None, mib=56):
    if cid is None:
        return pltpu.CompilerParams(vmem_limit_bytes=mib * 2**20)
    return pltpu.CompilerParams(
        collective_id=cid, has_side_effects=True, vmem_limit_bytes=mib * 2**20
    )


def start_kernel(x_ref, small_ref, qkv_ref, out_ref, all_small, w_ref, *sems):
    small_sends, small_recvs, sends, recvs = sems[:4]
    where = place()
    greet(where, PEERS + REP_NEIGHBOURS)
    me = shard_at(where)

    def small(n, offset, arriving=False):
        owner = shard_at(where, negative(offset)) if arriving else me
        return remote(
            small_ref, all_small.at[owner], small_sends, small_recvs, n, device(where, offset)
        )

    for n, offset in enumerate(PEERS):
        small(n, offset).start()
    all_small[me] = small_ref[...]
    spread = Spread(where, qkv_cuts(qkv_ref, rep_at(where)), w_ref, *sems[4:])
    spread.begin()
    for n, offset in enumerate(PEERS):
        small(n, offset, True).wait_recv()
    normed, _, _ = normalize(
        x_ref[...].astype(F32), small_row(all_small, 0), small_row(all_small, 1)
    )
    out_ref[me] = normed.astype(BF)
    gather = Gather(where, out_ref, sends, recvs)
    early = [i for i in TURNS if MOVES[i][3] is None]
    for i in early:
        gather.turn(i)
    spread.middle()
    queue = [("s", SLABS[i][4] - 1.5, i) for i in range(SLAB_COUNT)]
    queue += [("g", MOVES[i][4], i) for i in range(COUNT) if i not in early]
    for kind, _, i in sorted(queue, key=lambda e: e[1]):
        (spread if kind == "s" else gather).turn(i)
    gather.finish()
    spread.finish()
    for n, offset in enumerate(PEERS):
        small(n, offset).wait_send()


def start(x, small, qkv_weight):
    return pl.pallas_call(
        start_kernel,
        out_shape=(
            jax.ShapeDtypeStruct((GROUP, ROWS, WIDTH), BF),
            jax.ShapeDtypeStruct((GROUP, 8, LOCAL), F32),
            jax.ShapeDtypeStruct((GROUP, REPS, SLAB, 3 * LOCAL), BF),
        ),
        in_specs=[VM, VM, ANY],
        out_specs=(VM, VM, VM),
        scratch_shapes=[DMA((7,)), DMA((7,)), DMA((COUNT,)), DMA((COUNT,))] + spread_scratch(3),
        compiler_params=params(0),
        name="start",
    )(x, small, qkv_weight)


def attention_kernel(tokens_ref, w_ref, small_ref, table_ref, ow_ref, q_ref, k_ref, v_ref, att_ref, lse_ref, part_ref, vt_ref, mixed_ref):
    shard = lax.axis_index("shard")
    project(shard, tokens_ref, w_ref, small_ref, table_ref, q_ref, k_ref, v_ref)
    attend(q_ref, k_ref, v_ref, vt_ref, mixed_ref, att_ref, lse_ref)
    times(att_ref, ow_ref, part_ref)


def attention(tokens, w_qkv, small, table, out_weight):
    sds = jax.ShapeDtypeStruct
    return pl.pallas_call(
        attention_kernel,
        out_shape=(
            *[sds((TOTAL, LOCAL), BF)] * 4,
            sds((8, TOTAL), F32),
            sds((GROUP, ROWS, WIDTH), BF),
        ),
        in_specs=[VM] * 5,
        out_specs=(VM,) * 6,
        scratch_shapes=[pltpu.VMEM((LOCAL, TOTAL), BF), pltpu.VMEM((LOCAL, TOTAL), F32)],
        compiler_params=params(),
        name="attention",
    )(tokens, w_qkv, small, table, out_weight)


def middle_kernel(part_ref, x_ref, small_ref, gate_ref, up_ref, mid_ref, out_ref, w_ref, buf, land, *sems):
    back_sends, back_recvs, sends, recvs = sems[:4]
    where = place()
    greet(where, PEERS + REP_NEIGHBOURS)
    me = shard_at(where)
    spread = Spread(where, gate_up_cuts(gate_ref, up_ref, rep_at(where)), w_ref, *sems[4:])
    buf[...] = part_ref[...]
    scatter = Scatter(where, buf, land, back_sends, back_recvs)
    turns = [i for i in reversed(TURNS)]
    first = [i for i in turns if not FED[i]]
    for i in first:
        scatter.turn(i)
    spread.begin()
    rest = [i for i in turns if FED[i]]
    for i in rest[:4]:
        scatter.turn(i)
    spread.middle()
    early = [i for i in SLAB_TURNS if SLABS[i][3] is None]
    for i in early:
        spread.turn(i)
    for i in rest[4:]:
        scatter.turn(i)
    scatter.finish()
    mid = x_ref[...].astype(F32) + buf[me].astype(F32)
    mid_ref[...] = mid
    normed, _, _ = normalize(mid, small_row(small_ref, 2), small_row(small_ref, 3))
    out_ref[me] = normed.astype(BF)
    gather = Gather(where, out_ref, sends, recvs)
    starts = [i for i in TURNS if MOVES[i][3] is None]
    for i in starts:
        gather.turn(i)
    queue = [("s", SLABS[i][4] - 1, i) for i in range(SLAB_COUNT) if i not in early]
    queue += [("g", MOVES[i][4], i) for i in range(COUNT) if i not in starts]
    for kind, _, i in sorted(queue, key=lambda e: e[1]):
        (spread if kind == "s" else gather).turn(i)
    gather.finish()
    spread.finish()


def middle(part, x, small, gate_weight, up_weight):
    sds = jax.ShapeDtypeStruct
    return pl.pallas_call(
        middle_kernel,
        out_shape=(
            sds((ROWS, WIDTH), F32),
            sds((GROUP, ROWS, WIDTH), BF),
            sds((GROUP, REPS, SLAB, 2 * HID), BF),
        ),
        in_specs=[VM, VM, VM, ANY, ANY],
        out_specs=(VM, VM, VM),
        scratch_shapes=[
            pltpu.VMEM((GROUP, ROWS, WIDTH), BF),
            pltpu.VMEM((LANDINGS, ROWS, WIDTH // 2), BF),
            *[DMA((COUNT,))] * 4,
        ]
        + spread_scratch(2),
        compiler_params=params(1),
        name="middle",
    )(part, x, small, gate_weight, up_weight)


def mlp_kernel(tokens_ref, grads_ref, w_ref, down_ref, hid_ref, dgu_ref, part_ref, back_ref):
    shard = lax.axis_index("shard")
    feed_forward(shard, tokens_ref, grads_ref, w_ref, down_ref, hid_ref, dgu_ref)
    times(hid_ref, down_ref, part_ref)
    times_back(dgu_ref, w_ref, back_ref)


def mlp(tokens, grads, w_gu, down):
    sds = jax.ShapeDtypeStruct
    return pl.pallas_call(
        mlp_kernel,
        out_shape=(
            sds((TOTAL, HID), BF),
            sds((TOTAL, 2 * HID), BF),
            sds((GROUP, ROWS, WIDTH), BF),
            sds((GROUP, ROWS, WIDTH), BF),
        ),
        in_specs=[VM] * 4,
        out_specs=(VM,) * 4,
        compiler_params=params(),
        name="mlp",
    )(tokens, grads, w_gu, down)


def turnback_kernel(part_ref, mid_ref, gy_ref, small_ref, a2_ref, dgu_ref, hid_ref, grads_ref, dmid_ref, out_ref, sums_ref, ggu_ref, gdown_ref, buf, land, *sems):
    back_sends, back_recvs, sends, recvs = sems[:4]
    where = place()
    greet(where, NEIGHBOURS)
    me = shard_at(where)
    buf[...] = part_ref[...]
    scatter = Scatter(where, buf, land, back_sends, back_recvs)
    for i in reversed(TURNS):
        scatter.turn(i)
    scatter.finish()
    gain = small_row(small_ref, 2)
    _, scaled, inverse = normalize(mid_ref[...], gain, small_row(small_ref, 3))
    grad = buf[me].astype(F32)
    sums_ref[0:1, :] = jnp.sum(grad * scaled, 0, keepdims=True)
    sums_ref[1:2, :] = jnp.sum(grad, 0, keepdims=True)
    dmid = gy_ref[...].astype(F32) + normalize_back(grad, gain, scaled, inverse)
    dmid_ref[...] = dmid
    out_ref[me] = dmid.astype(BF)
    gather = Gather(where, out_ref, sends, recvs)
    starts = [i for i in TURNS if MOVES[i][3] is None]
    for i in starts:
        gather.turn(i)
    outer(hid_ref, grads_ref, gdown_ref)
    for i in TURNS:
        if i not in starts:
            gather.turn(i)
    outer(a2_ref, dgu_ref, ggu_ref)
    gather.finish()


def turnback(part, mid, gy, small, a2, dgu, hid, grads):
    sds = jax.ShapeDtypeStruct
    return pl.pallas_call(
        turnback_kernel,
        out_shape=(
            sds((ROWS, WIDTH), F32),
            sds((GROUP, ROWS, WIDTH), BF),
            sds((8, WIDTH), F32),
            sds((WIDTH, 2 * HID), BF),
            sds((HID, WIDTH), BF),
        ),
        in_specs=[VM] * 8,
        out_specs=(VM,) * 5,
        scratch_shapes=[
            pltpu.VMEM((GROUP, ROWS, WIDTH), BF),
            pltpu.VMEM((LANDINGS, ROWS, WIDTH // 2), BF),
            *[DMA((COUNT,))] * 4,
        ],
        compiler_params=params(2, 60),
        name="turnback",
    )(part, mid, gy, small, a2, dgu, hid, grads)


def attention_back_kernel(tokens_ref, ow_ref, q_ref, k_ref, v_ref, lse_ref, table_ref, w_ref, att_ref, dqkv_ref, part_ref, sums_ref, gout_ref, da_ref, kt_ref, dqt_ref, dk_ref, dv_ref):
    @pl.loop(0, CHUNKS)
    def _(i):
        da_ref[chunk_rows(i), :] = dot_nt(token_chunk(tokens_ref, i), ow_ref[...]).astype(BF)

    attend_back(q_ref, k_ref, v_ref, da_ref, lse_ref, kt_ref, dqt_ref, dk_ref, dv_ref)
    sums_ref[...] = jnp.zeros_like(sums_ref)
    for i in range(CHUNKS):
        rows = slice(i * CHUNK, (i + 1) * CHUNK)
        grad_q = dqt_ref[:, rows].T * HEAD_DIM ** (-0.5)
        for j, value in enumerate((grad_q, dk_ref[rows, :], dv_ref[rows, :])):
            if j < 2:
                value = turned(value, table_ref, rows, -1)
            low = value.astype(BF)
            cols = slice(j * LOCAL, (j + 1) * LOCAL)
            dqkv_ref[rows, cols] = low
            sums_ref[0:1, cols] += jnp.sum(low.astype(F32), 0, keepdims=True)
    times_back(dqkv_ref, w_ref, part_ref)
    outer(att_ref, tokens_ref, gout_ref)


def attention_back(tokens, out_weight, q, k, v, lse, table, w_qkv, att):
    sds = jax.ShapeDtypeStruct
    return pl.pallas_call(
        attention_back_kernel,
        out_shape=(
            sds((TOTAL, 3 * LOCAL), BF),
            sds((GROUP, ROWS, WIDTH), BF),
            sds((8, 3 * LOCAL), F32),
            sds((LOCAL, WIDTH), BF),
        ),
        in_specs=[VM] * 9,
        out_specs=(VM,) * 4,
        scratch_shapes=[
            pltpu.VMEM((TOTAL, LOCAL), BF),
            pltpu.VMEM((LOCAL, TOTAL), BF),
            pltpu.VMEM((LOCAL, TOTAL), F32),
            pltpu.VMEM((TOTAL, LOCAL), F32),
            pltpu.VMEM((TOTAL, LOCAL), F32),
        ],
        compiler_params=params(),
        name="attention_back",
    )(tokens, out_weight, q, k, v, lse, table, w_qkv, att)


def finish_kernel(part_ref, x_ref, dmid_ref, small_ref, a1_ref, dqkv_ref, down_ref, mid_ref, grad_ref, act_ref, sums_ref, gqkv_ref, buf, land, buf_down, land_down, *sems):
    where = place()
    greet(where, NEIGHBOURS)
    me = shard_at(where)
    buf[...] = part_ref[...]
    buf_down[...] = down_ref[...]
    scatter = Scatter(where, buf, land, sems[0], sems[1])
    first = [i for i in reversed(TURNS) if not FED[i]]
    for i in first:
        scatter.turn(i)
    outer(a1_ref, dqkv_ref, gqkv_ref)
    for i in reversed(TURNS):
        if i not in first:
            scatter.turn(i)
    scatter.finish()
    gain = small_row(small_ref, 0)
    _, scaled, inverse = normalize(x_ref[...].astype(F32), gain, small_row(small_ref, 1))
    grad = buf[me].astype(F32)
    sums_ref[0:1, :] = jnp.sum(grad * scaled, 0, keepdims=True)
    sums_ref[1:2, :] = jnp.sum(grad, 0, keepdims=True)
    grad_ref[...] = dmid_ref[...] + normalize_back(grad, gain, scaled, inverse)
    last = Scatter(where, buf_down, land_down, sems[2], sems[3])
    last.run()
    act_ref[...] = (mid_ref[...] + buf_down[me].astype(F32)).astype(BF)


def finish(part, x, dmid, small, a1, dqkv, down, mid):
    sds = jax.ShapeDtypeStruct
    return pl.pallas_call(
        finish_kernel,
        out_shape=(
            sds((ROWS, WIDTH), F32),
            sds((ROWS, WIDTH), BF),
            sds((8, WIDTH), F32),
            sds((WIDTH, 3 * LOCAL), BF),
        ),
        in_specs=[VM] * 8,
        out_specs=(VM,) * 4,
        scratch_shapes=[
            pltpu.VMEM((GROUP, ROWS, WIDTH), BF),
            pltpu.VMEM((LANDINGS, ROWS, WIDTH // 2), BF),
            pltpu.VMEM((GROUP, ROWS, WIDTH), BF),
            pltpu.VMEM((LANDINGS, ROWS, WIDTH // 2), BF),
            *[DMA((COUNT,))] * 4,
        ],
        compiler_params=params(3),
        name="finish",
    )(part, x, dmid, small, a1, dqkv, down, mid)


class Return:
    def __init__(self, where, ref, out, first_sends, first_recvs, sends, recvs):
        self.where, self.ref, self.out = where, ref, out
        self.first_sends, self.first_recvs = first_sends, first_recvs
        self.slabs = SlabGather(where, out, sends, recvs)

    def first(self, n, offset, arriving=False):
        me, rep = shard_at(self.where), rep_at(self.where)
        source = shard_at(self.where, negative(offset)) if arriving else me
        return remote(
            self.ref.at[shard_at(self.where, offset), rep],
            self.out.at[source, rep],
            self.first_sends,
            self.first_recvs,
            n,
            device(self.where, offset),
        )

    def begin(self):
        me, rep = shard_at(self.where), rep_at(self.where)
        for n, offset in enumerate(PEERS):
            self.first(n, offset).start()
        self.out[me, rep] = self.ref[me, rep]

    def middle(self):
        for n, offset in enumerate(PEERS):
            self.first(n, offset, True).wait_recv()

    def finish(self):
        self.slabs.finish()
        for n, offset in enumerate(PEERS):
            self.first(n, offset).wait_send()


class Vectors:
    ROUNDS = ((TWIN,), (NEAR,), (NORTH, SOUTH, (0, 0, 0, 2, 0)))

    def __init__(self, where, msg, land, mine, round_land, first_sends, first_recvs, sends, recvs):
        self.where, self.msg, self.land, self.mine, self.round_land = where, msg, land, mine, round_land
        self.first_sends, self.first_recvs = first_sends, first_recvs
        self.sends, self.recvs = sends, recvs

    def first(self, n, offset, arriving=False):
        me = shard_at(self.where)
        source = shard_at(self.where, negative(offset)) if arriving else me
        return remote(
            self.msg.at[shard_at(self.where, offset)],
            self.land.at[source],
            self.first_sends,
            self.first_recvs,
            n,
            device(self.where, offset),
        )

    def begin(self):
        me = shard_at(self.where)
        for n, offset in enumerate(PEERS):
            self.first(n, offset).start()
        self.land[me] = self.msg[me]

    def middle(self):
        me = shard_at(self.where)
        for n, offset in enumerate(PEERS):
            self.first(n, offset, True).wait_recv()
        total = self.land[0]
        for source in range(1, GROUP):
            total = total + self.land[source]
        self.mine[0] = total
        for p in range(3):
            block = 3 * me + p
            self.mine[0, 4 + p : 5 + p, :] = self.land[lax.rem(block, GROUP), pl.ds(4 + block // GROUP, 1), :]

    def hop(self, n, i, step):
        return remote(self.mine.at[n], self.round_land.at[i], self.sends, self.recvs, i, device(self.where, step))

    def round(self, n):
        base = sum(len(r) for r in self.ROUNDS[:n])
        for i, step in enumerate(self.ROUNDS[n]):
            self.hop(n, base + i, step).start()
        total = self.mine[n]
        for i, step in enumerate(self.ROUNDS[n]):
            self.hop(n, base + i, step).wait_recv()
            total = total + self.round_land[base + i]
        self.mine[n + 1] = total

    def finish(self):
        for n, offset in enumerate(PEERS):
            self.first(n, offset).wait_send()
        for n, steps in enumerate(self.ROUNDS):
            base = sum(len(r) for r in self.ROUNDS[:n])
            for i, step in enumerate(steps):
                self.hop(n, base + i, step).wait_send()


VECTOR_SCRATCH = [
    pltpu.VMEM((GROUP, 8, LOCAL), F32),
    pltpu.VMEM((GROUP, 8, LOCAL), F32),
    pltpu.VMEM((4, 8, LOCAL), F32),
    pltpu.VMEM((5, 8, LOCAL), F32),
    DMA((7,)),
    DMA((7,)),
    DMA((5,)),
    DMA((5,)),
]


class Writer:
    def __init__(self, stage, sem):
        self.stage, self.sem, self.count, self.flying = stage, sem, 0, []

    def put(self, value, dst):
        slot = self.count % 2
        if self.count >= 2:
            self.flying.pop(0).wait()
        rows, cols = value.shape
        src = self.stage.at[slot, pl.ds(0, rows), pl.ds(0, cols)]
        self.stage[slot, :rows, :cols] = value
        copy = pltpu.make_async_copy(src, dst, self.sem.at[slot])
        copy.start()
        self.flying.append(copy)
        self.count += 1

    def finish(self):
        for copy in self.flying:
            copy.wait()


def unpack_columns(block, out_ref, writer, base, width, starts):
    for s in range(GROUP):
        value = block(s)
        start = starts[s]
        if s % 2 == 0:
            seam = value[:, 640:] + block(s + 1)[:, :128]
            value = jnp.concatenate([value[:, :640], seam], axis=1)
        else:
            value, start = value[:, 128:], start + 128
        writer.put(value, out_ref.at[:, pl.ds(start, value.shape[1])])


def reduce_kernel(ggu_ref, grest_ref, gqkv_ref, one_ref, two_ref, bias_ref, gate_ref, up_ref, qkv_ref, rest_ref, vec_ref, *scratch):
    where = place()
    greet(where, PEERS + REP_NEIGHBOURS + ((0, 0, 0, 2, 0),))
    me, rep = shard_at(where), rep_at(where)
    refs = (ggu_ref, grest_ref, gqkv_ref)
    copies, lands, outs = scratch[0:3], scratch[3:6], scratch[6:9]
    sems = scratch[9:]
    scatters = [
        SlabScatter(where, copies[n], lands[n], sems[4 * n], sems[4 * n + 1]) for n in range(3)
    ]
    vectors = Vectors(where, *sems[16:24])
    stage, stage_sem = sems[24:26]
    for d in range(GROUP):
        cols = slice(d * LOCAL, (d + 1) * LOCAL)
        vectors.msg[d, 0:2, :] = one_ref[0:2, cols]
        vectors.msg[d, 2:4, :] = two_ref[0:2, cols]
        for j in range(3):
            vectors.msg[d, 4 + j : 5 + j, :] = bias_ref[0:1, j * LOCAL : (j + 1) * LOCAL]
    vectors.begin()
    for n in range(3):
        copies[n][...] = refs[n][...]
        for i in reversed(SLAB_TURNS):
            if not SLAB_FED[i]:
                scatters[n].turn(i)
    vectors.middle()
    for n in range(3):
        for i in reversed(SLAB_TURNS):
            if SLAB_FED[i]:
                scatters[n].turn(i)
        if n < 3:
            vectors.round(n)
    vec_ref[...] = vectors.mine[3]
    first = {0: sems[12:14], 2: sems[14:16]}
    gathers = []
    for n in range(3):
        scatters[n].finish()
        if n == 1:
            outs[n][:, rep] = copies[n][:, rep]
            gathers.append(SlabGather(where, outs[n], sems[4 * n + 2], sems[4 * n + 3]))
        else:
            back = Return(where, copies[n], outs[n], *first[n], sems[4 * n + 2], sems[4 * n + 3])
            back.begin()
            gathers.append(back)
    for n in range(3):
        if n != 1:
            gathers[n].middle()
        slabs = gathers[n] if n == 1 else gathers[n].slabs
        for i in SLAB_TURNS:
            slabs.turn(i)
    writer = Writer(stage, stage_sem)
    for n in range(3):
        gathers[n].finish()
        if n == 0:
            starts = [(s // 2) * 2 * LOCAL_FF + (s % 2) * 640 for s in range(GROUP)]
            for side, ref in enumerate((gate_ref, up_ref)):
                unpack_columns(
                    lambda s: outs[0][s, :, :, side * HID : (side + 1) * HID].reshape(LOCAL, HID).astype(F32),
                    ref, writer, 0, HID, starts,
                )
        elif n == 1:
            for j in range(4):
                for half in range(2):
                    cols = slice(half * 1024, (half + 1) * 1024)
                    writer.put(
                        outs[1][j, :, :, cols].reshape(LOCAL, 1024).astype(F32),
                        rest_ref.at[pl.ds(j * LOCAL, LOCAL), pl.ds(half * 1024, 1024)],
                    )
        else:
            for s in range(GROUP):
                for j in range(3):
                    writer.put(
                        outs[2][s, :, :, j * LOCAL : (j + 1) * LOCAL].reshape(LOCAL, LOCAL).astype(F32),
                        qkv_ref.at[:, pl.ds(j * WIDTH + s * LOCAL, LOCAL)],
                    )
    writer.finish()
    vectors.finish()


def reduce(g_gu, g_rest, g_qkv, sums_one, sums_two, sums_bias):
    sds = jax.ShapeDtypeStruct
    shapes = [(GROUP, REPS, SLAB, 2 * HID), (4, REPS, SLAB, WIDTH), (GROUP, REPS, SLAB, 3 * LOCAL)]
    return pl.pallas_call(
        reduce_kernel,
        out_shape=(
            sds((LOCAL, FF), F32),
            sds((LOCAL, FF), F32),
            sds((LOCAL, 3 * WIDTH), F32),
            sds((4 * LOCAL, WIDTH), F32),
            sds((8, LOCAL), F32),
        ),
        in_specs=[VM] * 6,
        out_specs=(ANY, ANY, ANY, ANY, VM),
        scratch_shapes=[pltpu.VMEM(s, BF) for s in shapes]
        + [pltpu.VMEM((SLAB_LANDINGS, s[0], SLAB, s[3]), BF) for s in shapes]
        + [pltpu.VMEM(s, BF) for s in shapes]
        + [DMA((SLAB_COUNT,))] * 12
        + [DMA((7,))] * 4
        + VECTOR_SCRATCH
        + [pltpu.VMEM((2, LOCAL, 1024), F32), DMA((2,))],
        compiler_params=params(4, 62),
        name="reduce",
    )(g_gu.reshape(shapes[0]), g_rest.reshape(shapes[1]), g_qkv.reshape(shapes[2]), sums_one, sums_two, sums_bias)


def shards(
    inputs,
    cotangent,
    ln1_gain,
    ln1_bias,
    qkv_weight,
    qkv_bias,
    out_weight,
    ln2_gain,
    ln2_bias,
    gate_weight,
    up_weight,
    down_weight,
):
    batch, length, width = inputs.shape
    me = lax.axis_index("shard")
    odd = lax.rem(me, 2)
    table = jnp.asarray(rotary_tables())
    x = inputs.reshape(length, width)
    gy = cotangent.reshape(length, width)
    rows = [ln1_gain, ln1_bias, ln2_gain, ln2_bias, qkv_bias, jnp.zeros((LOCAL,), BF)]
    small = jnp.concatenate(rows).astype(F32).reshape(8, LOCAL)
    grads = lax.all_gather(gy, "shard", axis=0)
    down = lax.dynamic_update_slice(jnp.zeros((HID, width), BF), down_weight, (64 * odd, 0))

    a1, all_small, w_qkv = start(x, small, qkv_weight)
    q, k, v, att, lse, part = attention(a1, w_qkv, all_small, table, out_weight)
    mid, a2, w_gu = middle(part, x, all_small, gate_weight, up_weight)
    hid, dgu, part_down, part_two = mlp(a2, grads, w_gu, down)
    dmid, dy1, sums_two, g_gu, g_down = turnback(part_two, mid, gy, all_small, a2, dgu, hid, grads)
    dqkv, part_one, sums_bias, g_out = attention_back(
        dy1, out_weight, q, k, v, lse, table, w_qkv, att
    )
    input_grad, activations, sums_one, g_qkv = finish(
        part_one, x, dmid, all_small, a1, dqkv, part_down, mid
    )

    g_rest = jnp.concatenate([g_out, g_down])
    g_gate, g_up, g_qkv, g_rest, vectors = reduce(g_gu, g_rest, g_qkv, sums_one, sums_two, sums_bias)
    g_down = lax.dynamic_slice(g_rest, (LOCAL + 64 * odd, 0), (LOCAL_FF, width))
    return (
        activations.reshape(batch, length, width),
        input_grad.reshape(batch, length, width),
        vectors[0],
        vectors[1],
        g_qkv,
        vectors[4:7].reshape(3 * LOCAL),
        g_rest[:LOCAL],
        vectors[2],
        vectors[3],
        g_gate,
        g_up,
        g_down,
    )


def solution(mesh):
    tokens, vector, matrix = P("rep", "shard", None), P("shard"), P("shard", None)
    return jax.shard_map(
        shards,
        mesh=mesh,
        in_specs=(tokens, tokens, vector, vector, matrix, vector, matrix, vector, vector, matrix, matrix, matrix),
        out_specs=(tokens, tokens, vector, vector, matrix, vector, matrix, vector, vector, matrix, matrix, matrix),
        check_vma=False,
    )
```

time: 2760 us -> 599 us (0.22)
  the two profiles are of different devices: /device:TPU:3 before, /device:TPU:8 now
where the time goes in v1:
time: 599 us; the launch traced here: 591 us
  Pallas kernels  540 us (90%)
  local copies, waits for them, and re-layouts  31.6 us (5%)
  between operations  14.6 us (2%)
    pallas_call x1, Pallas kernels, reduce(): pl.pallas_call(reduce_kernel, out_shape=(sds((LOCAL, FF), F32), sds((LOCA...  163 us
    pallas_call x1, Pallas kernels, middle(): pl.pallas_call(middle_kernel, out_shape=(sds((ROWS, WIDTH), F32), sds((GR...  82.3 us
    pallas_call x1, Pallas kernels, turnback(): pl.pallas_call(turnback_kernel, out_shape=(sds((ROWS, WIDTH), F32), sds((...  81.2 us
    pallas_call x1, Pallas kernels, start(): pl.pallas_call(start_kernel, out_shape=(jax.ShapeDtypeStruct((GROUP, ROWS...  67.9 us
    pallas_call x1, Pallas kernels, finish(): pl.pallas_call(finish_kernel, out_shape=(sds((ROWS, WIDTH), F32), sds((RO...  63 us
    pallas_call x1, Pallas kernels, mlp(): pl.pallas_call(mlp_kernel, out_shape=(sds((TOTAL, HID), BF), sds((TOTAL,...  31.4 us
    pallas_call x1, Pallas kernels, attention_back(): pl.pallas_call(attention_back_kernel, out_shape=(sds((TOTAL, 3 * LOCAL),...  27.2 us
    pallas_call x1, Pallas kernels, attention(): pl.pallas_call(attention_kernel, out_shape=(*[sds((TOTAL, LOCAL), BF)] *...  24 us
  transfers between devices with their start and end apart: 1, of which 0 were waited for; matrix products, arithmetic and copies ran while one was open for 1% of the time, Pallas kernels for 29%

profile of v1, /device:TPU:8, one launch (start us, length us, event | category | flops | bytes accessed | tf_op | source)
XLA Modules:
  0.0 590.8 jit_solution(9238099583666824064)
XLA Ops:
  7.2 0.0 all-gather.2.cloned.1.call-start
  7.2 0.7 all-gather.2.cloned.1.call-update
  7.9 0.9 dynamic-update-slice
  8.8 0.8 dynamic-update-slice.1
  9.6 0.8 dynamic-update-slice.2
  10.5 0.8 dynamic-update-slice.3
  11.3 0.8 dynamic-update-slice.4
  12.1 0.2 dynamic-update-slice.5
  12.4 0.6 reshape.60.small_ref
  13.0 67.9 %start.1 = (bf16[8,128,2048]{2,1,0:T(8,128)(2,1)}, f32[8,8,256]{2,1,0:T(8,128)}, bf16[8,16,16,768]{3,2,1,0:T(8,128)(2,1)}) custom-call(bf16[128,2048]{1,0:T(8,128)(2,1)} %bitcast.19, f32[8,256]{1,0:T(8,128)} %reshape.60.small_ref, bf16[256,6144]{1,0:T(8,128)(2,1)} %qkv_ref.1), custom_call_target="tpu_custom_call" | custom-call | tf_op jit(solution)/shard_map/start/pallas_call | solution.py:681
  80.9 24.0 %attention.1 = (bf16[1024,256]{1,0:T(8,128)(2,1)}, bf16[1024,256]{1,0:T(8,128)(2,1)}, bf16[1024,256]{1,0:T(8,128)(2,1)}, bf16[1024,256]{1,0:T(8,128)(2,1)}, f32[...) custom-call(bf16[8,128,2048]{2,1,0:T(8,128)(2,1)} %get-tuple-element.46.tokens_ref.a1_ref, ...), custom_call_target="tpu_custom_call" | custom-call | tf_op jit(solution)/shard_map/attention/pallas_call | solution.py:705
  104.9 82.3 %middle.1 = (f32[128,2048]{1,0:T(8,128)}, bf16[8,128,2048]{2,1,0:T(8,128)(2,1)}, bf16[8,16,16,1536]{3,2,1,0:T(8,128)(2,1)}) custom-call(bf16[8,128,2048]{2,1,0:T(8,128)(2,1)} %get-tuple-element.49.part_ref, bf16[128,2048]{1,0:T(8,128)(2,1)} %bitcast.20, f32[8,8,256]{2,1,0:T(8,128)} %get-tuple-element.48.small_ref, bf16[256,5632]{1,0:T(8,128)(2,1)} %gate_ref.1, ...), custom_call_target="tpu_custom_call" | custom-call | tf_op jit(solution)/shard_map/middle/pallas_call | solution.py:761
  187.2 0.0 copy-start.2
  187.3 0.4 broadcast_in_dim.7
  187.6 1.4 copy-done.2
  189.1 0.4 constant_dynamic-update-slice_fusion.down_ref
  189.5 0.0 copy-start
  189.5 0.0 all-gather.2.cloned.1.call-done.grads_ref
  189.5 1.6 copy-done
  191.2 31.4 %mlp.1 = (bf16[1024,768]{1,0:T(8,128)(2,1)}, bf16[1024,1536]{1,0:T(8,128)(2,1)}, bf16[8,128,2048]{2,1,0:T(8,128)(2,1)}, bf16[8,128,2048]{2,1,0:T(8,128)(2,1)}) custom-call(bf16[8,128,2048]{2,1,0:T(8,128)(2,1)} %get-tuple-element.50.tokens_ref.a2_ref, bf16[8,128,2048]{2,1,0:T(8,128)(2,1)} %all-gather.2.cloned.1.call-done.grads_ref, ...), custom_call_target="tpu_custom_call" | custom-call | tf_op jit(solution)/shard_map/mlp/pallas_call | solution.py:790
  222.6 81.2 %turnback.1 = (f32[128,2048]{1,0:T(8,128)}, bf16[8,128,2048]{2,1,0:T(8,128)(2,1)}, f32[8,2048]{1,0:T(8,128)}, bf16[2048,1536]{1,0:T(8,128)(2,1)}, bf16[768,2048]{1,0:T(8,128)(2,1)}) custom-call(bf16[8,128,2048]{2,1,0:T(8,128)(2,1)} %get-tuple-element.52.part_ref, f32[128,2048]{1,0:T(8,128)} %get-tuple-element.53.mid_ref, bf16[128,2048]{1,0:T(8,128)(2,1)} %bitcast.23, ...), custom_call_target="tpu_custom_call" | custom-call | tf_op jit(solution)/shard_map/turnback/pallas_call | solution.py:837
  303.8 0.0 copy-start.1
  303.8 27.2 %attention_back.1 = (bf16[1024,768]{1,0:T(8,128)(2,1)}, bf16[8,128,2048]{2,1,0:T(8,128)(2,1)}, f32[8,768]{1,0:T(8,128)}, bf16[256,2048]{1,0:T(8,128)(2,1)}) custom-call(bf16[8,128,2048]{2,1,0:T(8,128)(2,1)} %get-tuple-element.56.tokens_ref, bf16[256,2048]{1,0:T(8,128)(2,1)} %ow_ref.3, bf16[1024,256]{1,0:T(8,128)(2,1)} %get-tuple-element.57.q_ref, ...), custom_call_target="tpu_custom_call" | custom-call | tf_op jit(solution)/shard_map/attention_back/pallas_call | solution.py:881
  331.1 0.0 copy-done.1
  331.1 3.8 pad_maximum_fusion
  334.9 63.0 %finish.1 = (f32[128,2048]{1,0:T(8,128)}, bf16[128,2048]{1,0:T(8,128)(2,1)}, f32[8,2048]{1,0:T(8,128)}, bf16[2048,768]{1,0:T(8,128)(2,1)}) custom-call(bf16[8,128,2048]{2,1,0:T(8,128)(2,1)} %get-tuple-element.62.part_ref, bf16[128,2048]{1,0:T(8,128)(2,1)} %bitcast.21, f32[128,2048]{1,0:T(8,128)} %get-tuple-element.63.dmid_ref, ...), custom_call_target="tpu_custom_call" | custom-call | tf_op jit(solution)/shard_map/finish/pallas_call | solution.py:931
  397.9 162.8 %reduce.1 = (f32[256,5632]{1,0:T(8,128)}, f32[256,5632]{1,0:T(8,128)}, f32[256,6144]{1,0:T(8,128)}, f32[1024,2048]{1,0:T(8,128)}, f32[8,256]{1,0:T(8,128)}) custom-call(bf16[8,16,16,1536]{3,2,1,0:T(8,128)(2,1)} %bitcast.12, bf16[4,16,16,2048]{3,2,1,0:T(8,128)(2,1)} %bitcast.11, bf16[8,16,16,768]{3,2,1,0:T(8,128)(2,1)} %bitcast.22, ...), custom_call_target="tpu_custom_call" | custom-call | tf_op jit(solution)/shard_map/reduce/pallas_call | solution.py:1173
  560.7 0.7 slice.20
  561.4 1.4 fusion
  562.8 0.6 reshape.59
  563.4 0.0 slice-start
  563.4 3.3 slice.21
  566.7 0.0 copy-start.4
  566.7 0.0 copy-start.3
  566.7 6.0 %constant_dynamic-slice_fusion = f32[704,2048]{1,0:T(8,128)} fusion(f32[1024,2048]{1,0:T(8,128)} %get-tuple-element.77, s32[]{:T(128)S(6)} %select_n.7), kind=kLoop, calls=%fused_computation.1 | loop fusion | bytes 11534340 | tf_op jit(solution)/shard_map/dynamic_slice | solution.py:1235
  572.8 0.0 copy-done.4
  572.8 0.8 copy.37
  573.6 0.0 copy-done.3
  573.6 1.0 copy.38
  574.5 0.0 slice-done
  574.5 0.0 slice-done.1
  574.6 3.2 copy.39
  577.8 0.0 slice-done.4
  577.8 0.0 slice-done.5
  577.8 2.6 copy.40
  580.4 0.0 slice-done.2
  580.4 0.5 slice-done.3
  580.9 2.5 copy.41
  (10 shorter events, 0.0 us)
Async XLA Ops:
  7.2 182.3 %all-gather.2.cloned.1.call-start = ((), (), s32[]{:S(2)}) async-start(), calls=%async_computation | async-start | bytes 4718592 | tf_op jit(solution)/shard_map/all_gather | solution.py:1218
  187.2 1.8 copy-start.2
  189.5 1.7 copy-start
  303.8 27.2 %copy-start.1 = (bf16[768,2048]{1,0:T(8,128)(2,1)S(1)}, bf16[768,2048]{1,0:T(8,128)(2,1)}, u32[]{:S(2)}) copy-start(bf16[768,2048]{1,0:T(8,128)(2,1)} %get-tuple-element.70) | copy-start | bytes 9437188
  563.4 11.1 %slice-start = ((s8[6291456]{0:T(1024)(128)(4,1)}), s8[4194304]{0:T(1024)(128)(4,1)S(1)}, s32[]{:S(2)}) async-start(s8[6291456]{0:T(1024)(128)(4,1)} %bitcast.13), calls=%async_computation.1 | async-start | bytes 8388608
  566.7 6.1 %copy-start.4 = (bf16[128,2048]{1,0:T(8,128)(2,1)S(1)}, bf16[128,2048]{1,0:T(8,128)(2,1)}, u32[]{:S(2)}) copy-start(bf16[128,2048]{1,0:T(8,128)(2,1)} %get-tuple-element.66) | copy-start | bytes 1572868
  566.7 6.9 %copy-start.3 = (f32[128,2048]{1,0:T(8,128)S(1)}, f32[128,2048]{1,0:T(8,128)}, u32[]{:S(2)}) copy-start(f32[128,2048]{1,0:T(8,128)} %get-tuple-element.67) | copy-start | bytes 3145732
  566.7 7.8 %slice-start.1 = ((s8[6291456]{0:T(1024)(128)(4,1)}), s8[2097152]{0:T(1024)(128)(4,1)S(1)}, s32[]{:S(2)}) async-start(s8[6291456]{0:T(1024)(128)(4,1)} %bitcast.13), calls=%async_computation.2 | async-start | bytes 4194304
  566.7 11.0 %slice-start.4 = ((s8[5767168]{0:T(1024)(128)(4,1)}), s8[4194304]{0:T(1024)(128)(4,1)S(1)}, s32[]{:S(2)}) async-start(s8[5767168]{0:T(1024)(128)(4,1)} %bitcast.17), calls=%async_computation.5 | async-start | bytes 8388608
  573.6 4.2 slice-start.5
  573.6 6.8 %slice-start.2 = ((s8[5767168]{0:T(1024)(128)(4,1)}), s8[4194304]{0:T(1024)(128)(4,1)S(1)}, s32[]{:S(2)}) async-start(s8[5767168]{0:T(1024)(128)(4,1)} %bitcast.15), calls=%async_computation.3 | async-start | bytes 8388608
  574.6 6.4 %slice-start.3 = ((s8[5767168]{0:T(1024)(128)(4,1)}), s8[1572864]{0:T(1024)(128)(4,1)S(1)}, s32[]{:S(2)}) async-start(s8[5767168]{0:T(1024)(128)(4,1)} %bitcast.15), calls=%async_computation.4 | async-start | bytes 3145728
Sparse Core Ops, SparseCore 0:
  10.4 87.3 all-gather.1

commit v2 on v1

v2 whole, which is shorter than its diff:
```python
import functools

import jax
import jax.numpy as jnp
import numpy as np
from jax import lax
from jax.experimental import pallas as pl
from jax.experimental.pallas import tpu as pltpu
from jax.sharding import PartitionSpec as P

HEADS = 32
HEAD_DIM = 64
ROT = 16
WIDTH = 2048
GROUP = 8
REPS = 16
ROWS = 128
TOTAL = GROUP * ROWS
LOCAL = WIDTH // GROUP
LOCAL_HEADS = HEADS // GROUP
FF = 5632
LOCAL_FF = FF // GROUP
HID = 768
SLAB = LOCAL // REPS
NEAR_COLS, FAR_COLS = 768, 1280
CHUNK = 256
CHUNKS = TOTAL // CHUNK
EPS = 1e-05
BASE = 10000.0
BF = jnp.bfloat16
F32 = jnp.float32
MESH = pl.DeviceIdType.MESH
VM = pl.BlockSpec(memory_space=pltpu.VMEM)
ANY = pl.BlockSpec(memory_space=pl.ANY)
DMA = pltpu.SemaphoreType.DMA


def dot(left, right):
    return jnp.dot(left, right, preferred_element_type=F32)


def dot_nt(left, right):
    return lax.dot_general(left, right, (((1,), (1,)), ((), ())), preferred_element_type=F32)


FAR, UP, DOWN = (1, 0, 0, 0, 0), (0, 1, 0, 0, 0), (0, -1, 0, 0, 0)
NEAR, NORTH, SOUTH, TWIN = (0, 0, 1, 0, 0), (0, 0, 0, 1, 0), (0, 0, 0, -1, 0), (0, 0, 0, 0, 1)
HERE = (0, 0, 0, 0, 0)
SIZES = (2, 4, 2, 4, 2)
PEERS = tuple((f, z, 0, 0, 0) for f in range(2) for z in range(4) if (f, z) != (0, 0))


def place():
    shard, rep = lax.axis_index("shard"), lax.axis_index("rep")
    return (shard // 4, lax.rem(shard, 4), rep // 8, lax.rem(rep // 2, 4), lax.rem(rep, 2))


def shift(where, offset):
    return tuple(
        lax.rem(a + (o + 2 * n) % n, n) if o % n else a for a, o, n in zip(where, offset, SIZES)
    )


def shard_at(where, offset=HERE):
    far, level = shift(where, offset)[:2]
    return far * 4 + level


def rep_at(where, offset=HERE):
    near, north, core = shift(where, offset)[2:]
    return near * 8 + north * 2 + core


def device(where, offset):
    return (shard_at(where, offset), rep_at(where, offset))


def less(a, b):
    return tuple((p - q) % n for p, q, n in zip(a, b, SIZES))


def negative(a):
    return tuple(-p for p in a)


def greet(where, offsets):
    barrier = pltpu.get_barrier_semaphore()
    for offset in offsets:
        pl.semaphore_signal(
            barrier, inc=1, device_id=device(where, negative(offset)), device_id_type=MESH
        )
    pl.semaphore_wait(barrier, len(offsets))


def remote(src, dst, sends, recvs, i, to):
    return pltpu.make_async_remote_copy(
        src_ref=src,
        dst_ref=dst,
        send_sem=sends.at[i],
        recv_sem=recvs.at[i],
        device_id=to,
        device_id_type=MESH,
    )


def token_moves():
    moves = []

    def add(owner, part, step, first, turn):
        moves.append((owner, part, step, first, turn))
        return len(moves) - 1

    near, far = (0, NEAR_COLS), (NEAR_COLS, FAR_COLS)
    whole, top, low = (0, ROWS), (0, ROWS // 2), (ROWS // 2, ROWS // 2)
    up2 = (0, 2, 0, 0, 0)
    up = add(HERE, (whole, near), UP, None, 0)
    down = add(HERE, (whole, near), DOWN, None, 0)
    add(HERE, (whole, near), FAR, None, 0.2)
    a = add(DOWN, (top, near), UP, up, 1)
    b = add(UP, (low, near), DOWN, down, 1)
    add(DOWN, (whole, near), FAR, up, 1.1)
    add(UP, (whole, near), FAR, down, 1.1)
    add(up2, (top, near), FAR, a, 2)
    add(up2, (low, near), FAR, b, 2)
    over = add(HERE, (whole, far), FAR, None, 0.1)
    up = add(HERE, (whole, far), UP, None, 1.1)
    down = add(HERE, (whole, far), DOWN, None, 1.1)
    add(DOWN, (top, far), UP, up, 3)
    add(UP, (low, far), DOWN, down, 3)
    up = add(FAR, (whole, far), UP, over, 2.5)
    down = add(FAR, (whole, far), DOWN, over, 2.5)
    add(tuple(p + q for p, q in zip(FAR, DOWN)), (top, far), UP, up, 4)
    add(tuple(p + q for p, q in zip(FAR, UP)), (low, far), DOWN, down, 4)
    return tuple(moves)


MOVES = token_moves()
COUNT = len(MOVES)
TURNS = tuple(sorted(range(COUNT), key=lambda i: MOVES[i][4]))
FED = tuple(tuple(j for j in range(COUNT) if MOVES[j][3] == i) for i in range(COUNT))
NEIGHBOURS = (FAR, UP, DOWN)
LANDS = {}
for _i in range(COUNT):
    pair = MOVES[_i][1][0][0] > 0
    LANDS[_i] = LANDS[_i - 1] if pair else len(set(LANDS.values()))
LANDINGS = len(set(LANDS.values()))


def token_part(ref, block, part):
    (row, rows), (col, cols) = part
    return ref.at[block, pl.ds(row, rows), pl.ds(col, cols)]


class Gather:
    def __init__(self, where, ref, sends, recvs, own=None):
        self.where, self.ref, self.sends, self.recvs, self.own = where, ref, sends, recvs, own
        self.got = set()

    def move(self, i, arriving=False):
        owner, part, step, _, _ = MOVES[i]
        block = shard_at(self.where, less(owner, step) if arriving else owner)
        ref = token_part(self.ref, block, part)
        src = ref
        if owner == HERE and self.own is not None and not arriving:
            src = token_part(self.own, 0, part)
        return remote(src, ref, self.sends, self.recvs, i, device(self.where, step))

    def take(self, i):
        if i not in self.got:
            self.got.add(i)
            self.move(i, True).wait_recv()

    def turn(self, i):
        if MOVES[i][3] is not None:
            self.take(MOVES[i][3])
        self.move(i).start()

    def take_all(self):
        for i in TURNS:
            self.take(i)

    def finish(self):
        for i in TURNS:
            self.take(i)
        for i in TURNS:
            self.move(i).wait_send()

    def run(self):
        for i in TURNS:
            self.turn(i)
        self.finish()


def agenda(mover, turns, start, unit, backwards=False):
    last = max(turns[i] for i in turns)
    return [
        (start + unit * ((last - t) if backwards else t), mover, i) for i, t in turns.items()
    ]


def slab_agenda(mover, start, unit):
    turns = mover.slabs.TURNS if hasattr(mover, "slabs") else mover.TURNS
    return [(start + unit * t, mover, i) for i, t in enumerate(turns)]


class Agenda:
    def __init__(self):
        self.items = []

    def add(self, items):
        self.items = sorted(self.items + items, key=lambda e: e[0])

    def until(self, time):
        while self.items and self.items[0][0] <= time:
            _, mover, i = self.items.pop(0)
            mover.turn(i)


TOKEN_TURNS = {i: MOVES[i][4] for i in range(COUNT)}


class Scatter:
    def __init__(self, where, buf, land, sends, recvs):
        self.where, self.buf, self.land, self.sends, self.recvs = where, buf, land, sends, recvs
        self.got = set()

    def move(self, i, arriving=False):
        owner, part, step, _, _ = MOVES[i]
        block = shard_at(self.where, owner if arriving else less(owner, step))
        (row, rows), (col, cols) = part
        return remote(
            token_part(self.buf, block, part),
            self.land.at[LANDS[i], pl.ds(row, rows), pl.ds(0, cols)],
            self.sends,
            self.recvs,
            i,
            device(self.where, negative(step)),
        )

    def take(self, i):
        if i in self.got:
            return
        self.got.add(i)
        owner, ((row, rows), (col, cols)), _, _, _ = MOVES[i]
        self.move(i, True).wait_recv()
        at = (shard_at(self.where, owner), pl.ds(row, rows), pl.ds(col, cols))
        total = self.buf[at].astype(F32) + self.land[LANDS[i], pl.ds(row, rows), pl.ds(0, cols)].astype(F32)
        self.buf[at] = total.astype(BF)

    def turn(self, i):
        for j in FED[i]:
            self.take(j)
        self.move(i).start()

    def take_all(self):
        for i in reversed(TURNS):
            self.take(i)

    def finish(self):
        for i in reversed(TURNS):
            self.take(i)
        for i in reversed(TURNS):
            self.move(i).wait_send()

    def run(self):
        for i in reversed(TURNS):
            self.turn(i)
        self.finish()


ALONG = ((0, 0, 0, 1, 0), (0, 0, 0, 3, 0), (0, 0, 0, 2, 0))
SLAB_HOPS = (NEAR,) + ALONG + ALONG + (TWIN,)
SLAB_COUNT = 10
REP_NEIGHBOURS = (NEAR, TWIN) + ALONG


def spot(where, offset=HERE):
    near, north = shift(where, offset)[2:4]
    return near * 4 + north


def both(a, b):
    return tuple(p + q for p, q in zip(a, b))


class Spread:
    def __init__(self, where, cuts, ref, own_sem, first_sends, first_recvs, sends, recvs):
        self.where, self.cuts, self.ref, self.own_sem = where, cuts, ref, own_sem
        self.first_sends, self.first_recvs = first_sends, first_recvs
        self.slabs = RingGather(where, ref, sends, recvs)

    def first(self, n, offset, arriving=False):
        me = shard_at(self.where)
        owner = shard_at(self.where, negative(offset)) if arriving else me
        copies = []
        for j, (src, (col, cols)) in enumerate(self.cuts(shard_at(self.where, offset))):
            copies.append(
                remote(
                    src,
                    self.ref.at[owner, spot(self.where), self.where[4], :, pl.ds(col, cols)],
                    self.first_sends,
                    self.first_recvs,
                    (n, j),
                    device(self.where, offset),
                )
            )
        return copies

    def own(self):
        me = shard_at(self.where)
        return [
            pltpu.make_async_copy(
                src,
                self.ref.at[me, spot(self.where), self.where[4], :, pl.ds(col, cols)],
                self.own_sem.at[j],
            )
            for j, (src, (col, cols)) in enumerate(self.cuts(me))
        ]

    def begin(self):
        for n, offset in enumerate(PEERS):
            for copy in self.first(n, offset):
                copy.start()
        for copy in self.own():
            copy.start()

    def middle(self):
        for copy in self.own():
            copy.wait()
        for n, offset in enumerate(PEERS):
            for copy in self.first(n, offset, True):
                copy.wait_recv()

    def finish(self, taken=False):
        self.slabs.finish(taken)
        for n, offset in enumerate(PEERS):
            for copy in self.first(n, offset):
                copy.wait_send()

    def turn(self, i):
        self.slabs.turn(i)


def slab_span(ref, first, count):
    size = ref.shape[0]
    start, stop = first * size // GROUP, (first + count) * size // GROUP
    return pl.ds(start, stop - start)


class SlabGather:
    TURNS = (0, 0.6, 4.2)

    def __init__(self, where, ref, sends, recvs):
        self.where, self.ref, self.sends, self.recvs = where, ref, sends, recvs
        self.done = 0

    def hop(self, i, arriving=False):
        step = SLAB_HOPS[i]
        core = self.where[4]
        if step == TWIN:
            part = self.ref.at[:, :, (1 - core) if arriving else core]
        else:
            base = NEAR if 4 <= i < 7 else HERE
            owner = both(base, negative(step)) if arriving else base
            part = self.ref.at[:, spot(self.where, owner), core]
        return remote(part, part, self.sends, self.recvs, i, device(self.where, step))

    def turn(self, stage):
        assert stage == self.done
        self.done += 1
        if stage == 0:
            for i in range(4):
                self.hop(i).start()
        elif stage == 1:
            self.hop(0, True).wait_recv()
            for i in range(4, 7):
                self.hop(i).start()
        else:
            for i in range(1, 7):
                self.hop(i, True).wait_recv()
            self.hop(7).start()

    def take_all(self):
        self.hop(7, True).wait_recv()

    def finish(self, taken=False):
        if not taken:
            self.take_all()
        for i in range(len(SLAB_HOPS)):
            self.hop(i).wait_send()


class RingGather:
    TURNS = (0, 0.6, 1.2, 2.3, 3.4)
    NORTH, SOUTH = ALONG[:2]
    HOPS = (
        (NEAR, HERE, 0),
        (NORTH, HERE, 0),
        (SOUTH, HERE, 0),
        (NORTH, NEAR, 0),
        (SOUTH, NEAR, 0),
        (NORTH, HERE, 1),
        (SOUTH, HERE, 1),
        (NORTH, NEAR, 1),
        (SOUTH, NEAR, 1),
        (TWIN, HERE, 2),
    )

    def __init__(self, where, ref, sends, recvs):
        self.where, self.ref, self.sends, self.recvs = where, ref, sends, recvs
        self.done = 0
        self.cut = ref.shape[0] - ref.shape[0] // 2

    def hop(self, i, arriving=False):
        (step, base, kind), core = self.HOPS[i], self.where[4]
        if kind == 2:
            part = self.ref.at[:, :, (1 - core) if arriving else core]
        else:
            owner = both(base, negative(step)) if kind else base
            if arriving:
                owner = both(owner, negative(step))
            blocks = slice(None)
            if kind:
                blocks = (
                    pl.ds(0, self.cut)
                    if step == self.NORTH
                    else pl.ds(self.cut, self.ref.shape[0] - self.cut)
                )
            part = self.ref.at[blocks, spot(self.where, owner), core]
        return remote(part, part, self.sends, self.recvs, i, device(self.where, step))

    def turn(self, stage):
        assert stage == self.done
        self.done += 1
        waits, starts = (
            ((), (0, 1, 2)),
            ((0,), (3, 4)),
            ((1, 2), (5, 6)),
            ((3, 4), (7, 8)),
            ((5, 6, 7, 8), (9,)),
        )[stage]
        for i in waits:
            self.hop(i, True).wait_recv()
        for i in starts:
            self.hop(i).start()

    def take_all(self):
        self.hop(9, True).wait_recv()

    def finish(self, taken=False):
        if not taken:
            self.take_all()
        for i in range(10):
            self.hop(i).wait_send()


class SlabScatter:
    TURNS = (0, 1.0, 5.5)

    def __init__(self, where, ref, twin, land, sends, recvs):
        self.where, self.ref, self.twin, self.land = where, ref, twin, land
        self.sends, self.recvs = sends, recvs
        self.done = 0

    def hop(self, i, arriving=False):
        step = SLAB_HOPS[i]
        core = self.where[4]
        if step == TWIN:
            src, dst = self.ref.at[:, :, 1 - core], self.twin
        else:
            base = NEAR if 4 <= i < 7 else HERE
            src = self.ref.at[:, spot(self.where, both(base, step)), core]
            dst = self.land.at[i]
        return remote(src, dst, self.sends, self.recvs, i, device(self.where, step))

    def add(self, at, lands):
        core = self.where[4]
        rows = self.ref.shape[0]

        @pl.loop(0, rows)
        def _(n):
            total = self.ref[n, at, core].astype(F32)
            for i in lands:
                total = total + self.land[i, n].astype(F32)
            self.ref[n, at, core] = total.astype(BF)

    def turn(self, stage):
        assert stage == self.done
        self.done += 1
        if stage == 0:
            self.hop(7).start()
        elif stage == 1:
            core = self.where[4]
            self.hop(7, True).wait_recv()
            rows = self.ref.shape[0]

            @pl.loop(0, rows)
            def _(n):
                total = self.ref[n, :, core].astype(F32) + self.twin[n].astype(F32)
                self.ref[n, :, core] = total.astype(BF)

            for i in range(1, 7):
                self.hop(i).start()
        else:
            for i in range(4, 7):
                self.hop(i, True).wait_recv()
            self.add(spot(self.where, NEAR), (4, 5, 6))
            self.hop(0).start()

    def close(self):
        for i in range(4):
            self.hop(i, True).wait_recv()
        self.add(spot(self.where), (0, 1, 2, 3))

    def finish(self):
        for i in range(len(SLAB_HOPS)):
            self.hop(i).wait_send()

    def total(self):
        return self.ref.at[:, spot(self.where), self.where[4]]


def scatter_scratch(n, cols):
    return [pltpu.VMEM((n, 8, SLAB, cols), BF), pltpu.VMEM((7, n, SLAB, cols), BF)]


def spread_scratch(cuts):
    return [DMA((cuts,)), DMA((7, cuts)), DMA((7, cuts)), DMA((SLAB_COUNT,)), DMA((SLAB_COUNT,))]


def qkv_cuts(w_ref, rep):
    rows = pl.ds(pl.multiple_of(rep * SLAB, SLAB), SLAB)

    def cuts(shard):
        return [
            (
                w_ref.at[rows, pl.ds(pl.multiple_of(j * WIDTH + shard * LOCAL, LOCAL), LOCAL)],
                (j * LOCAL, LOCAL),
            )
            for j in range(3)
        ]

    return cuts


def hidden_start(shard):
    return (shard // 2) * (2 * LOCAL_FF) + lax.rem(shard, 2) * (5 * 128)


def gate_up_cuts(gate_ref, up_ref, rep):
    rows = pl.ds(pl.multiple_of(rep * SLAB, SLAB), SLAB)

    def cuts(shard):
        cols = pl.ds(pl.multiple_of(hidden_start(shard), 128), HID)
        return [(gate_ref.at[rows, cols], (0, HID)), (up_ref.at[rows, cols], (HID, HID))]

    return cuts


def standardize(values):
    center = values - jnp.mean(values, -1, keepdims=True)
    inverse = lax.rsqrt(jnp.mean(center * center, -1, keepdims=True) + EPS)
    return (center * inverse, inverse)


def normalize(values, gain, shift_):
    scaled, inverse = standardize(values)
    return (scaled * gain + shift_, scaled, inverse)


def normalize_back(grad, gain, scaled, inverse):
    weighted = grad * gain
    return inverse * (
        weighted
        - jnp.mean(weighted, -1, keepdims=True)
        - scaled * jnp.mean(weighted * scaled, -1, keepdims=True)
    )


def small_row(small_ref, row):
    return jnp.concatenate([small_ref[s, row : row + 1, :] for s in range(GROUP)], axis=1)


def rotary_tables():
    positions = np.arange(TOTAL, dtype=np.float32)
    freqs = np.float32(BASE) ** (-np.arange(0, ROT, 2).astype(np.float32) / np.float32(ROT))
    angles = positions[:, None] * freqs[None, :].astype(np.float32)
    cosine, sine = np.cos(angles).astype(np.float32), np.sin(angles).astype(np.float32)
    half = ROT // 2
    one = np.ones((TOTAL, HEAD_DIM), np.float32)
    low, high = np.zeros((TOTAL, HEAD_DIM), np.float32), np.zeros((TOTAL, HEAD_DIM), np.float32)
    one[:, :half], one[:, half:ROT] = cosine, cosine
    low[:, :half] = -sine
    high[:, half:ROT] = sine
    return np.stack([np.concatenate([t, t], 1) for t in (one, low, high)])


def turned(values, table_ref, rows, sign):
    parts = []
    for side in range(2):
        part = values[:, side * 128 : (side + 1) * 128]
        swing = pltpu.roll(part, 128 - ROT // 2, 1) * table_ref[1, rows, :] + (
            pltpu.roll(part, ROT // 2, 1) * table_ref[2, rows, :]
        )
        straight = part * table_ref[0, rows, :]
        parts.append(straight + swing if sign > 0 else straight - swing)
    return jnp.concatenate(parts, axis=1)


def chunk_rows(i):
    return pl.ds(pl.multiple_of(i * CHUNK, CHUNK), CHUNK)


def token_chunk(ref, i):
    return ref[pl.ds(i * 2, 2)].reshape(CHUNK, WIDTH)


def bias_row(small_ref, shard, j):
    block = j * GROUP + shard
    return small_ref[block // 3, pl.ds(4 + lax.rem(block, 3), 1), :]


def project(shard, tokens_ref, w_ref, small_ref, table_ref, q_ref, k_ref, v_ref, first, last):
    @pl.loop(first, last, unroll=2)
    def _(i):
        rows = chunk_rows(i)
        tokens = token_chunk(tokens_ref, i)
        for j, ref in enumerate((q_ref, k_ref, v_ref)):
            w = w_ref[:, :, :, :, j * LOCAL : (j + 1) * LOCAL].reshape(WIDTH, LOCAL)
            value = dot(tokens, w) + bias_row(small_ref, shard, j)
            if j < 2:
                value = turned(value, table_ref, rows, 1)
            if j == 0:
                value = value * HEAD_DIM ** (-0.5)
            ref[rows, :] = value.astype(BF)


def head_lanes(h):
    return lax.broadcasted_iota(jnp.int32, (CHUNK, LOCAL), 1) // HEAD_DIM == h


def key_parts(i):
    last = (CHUNK * i, CHUNK * (i + 1), True)
    return ((0, CHUNK * i, False), last) if i else (last,)


def hide_later(values, hidden):
    shape = values.shape
    keys = lax.broadcasted_iota(jnp.int32, shape, 0)
    return jnp.where(keys <= lax.broadcasted_iota(jnp.int32, shape, 1), values, hidden)


def attend(q_ref, k_ref, v_ref, vt_ref, mixed_ref, att_ref, lse_ref, poll):
    vt_ref[...] = v_ref[...].astype(F32).T.astype(BF)
    for i in range(CHUNKS):
        cols = slice(CHUNK * i, CHUNK * (i + 1))

        @pl.loop(0, LOCAL_HEADS, unroll=LOCAL_HEADS)
        def _(h):
            query = jnp.where(head_lanes(h), q_ref[cols, :], jnp.zeros((), BF))
            lanes = pl.ds(pl.multiple_of(h * HEAD_DIM, HEAD_DIM), HEAD_DIM)
            scores = []
            for first, last, diagonal in key_parts(i):
                part = dot_nt(k_ref[first:last, :], query)
                scores.append(hide_later(part, -1e30) if diagonal else part)
            top = functools.reduce(jnp.maximum, [jnp.max(s, 0, keepdims=True) for s in scores])
            expo = [jnp.exp(s - top) for s in scores]
            denom = sum(jnp.sum(e, 0, keepdims=True) for e in expo)
            share = 1.0 / denom
            mixed_ref[lanes, cols] = sum(
                dot(vt_ref[lanes, first:last], (e * share).astype(BF))
                for e, (first, last, _) in zip(expo, key_parts(i))
            )
            lse_ref[pl.ds(h, 1), cols] = top + jnp.log(denom)

        att_ref[cols, :] = mixed_ref[:, cols].T.astype(BF)
        poll(i)


def attend_back(q_ref, k_ref, v_ref, da_ref, lse_ref, kt_ref, dqt_ref, dk_ref, dv_ref, poll):
    kt_ref[...] = k_ref[...].astype(F32).T.astype(BF)
    dk_ref[...] = jnp.zeros_like(dk_ref)
    dv_ref[...] = jnp.zeros_like(dv_ref)
    for i in range(CHUNKS):
        cols = slice(CHUNK * i, CHUNK * (i + 1))

        @pl.loop(0, LOCAL_HEADS, unroll=LOCAL_HEADS)
        def _(h):
            query = jnp.where(head_lanes(h), q_ref[cols, :], jnp.zeros((), BF))
            grad = jnp.where(head_lanes(h), da_ref[cols, :], jnp.zeros((), BF))
            lanes = pl.ds(pl.multiple_of(h * HEAD_DIM, HEAD_DIM), HEAD_DIM)
            top = lse_ref[pl.ds(h, 1), cols]
            probs, grad_probs = [], []
            for first, last, diagonal in key_parts(i):
                part = jnp.exp(dot_nt(k_ref[first:last, :], query) - top)
                probs.append(hide_later(part, 0.0) if diagonal else part)
                grad_probs.append(dot_nt(v_ref[first:last, :], grad))
            total = sum(jnp.sum(g * p, 0, keepdims=True) for g, p in zip(grad_probs, probs))
            pieces = []
            for p, g, (first, last, _) in zip(probs, grad_probs, key_parts(i)):
                grad_scores = (p * (g - total)).astype(BF)
                dv_ref[first:last, :] += dot(p.astype(BF), grad)
                dk_ref[first:last, :] += dot(grad_scores, query)
                pieces.append(dot(kt_ref[lanes, first:last], grad_scores))
            dqt_ref[lanes, cols] = sum(pieces)

        poll(i)


def times(left_ref, w_ref, out_ref, first=0, last=CHUNKS):
    @pl.loop(first, last, unroll=2)
    def _(i):
        left = left_ref[chunk_rows(i), :]
        for j in range(WIDTH // 512):
            cols = slice(j * 512, (j + 1) * 512)
            out_ref[pl.ds(i * 2, 2), :, cols] = (
                dot(left, w_ref[:, cols]).astype(BF).reshape(2, ROWS, 512)
            )


def times_back(left_ref, w_ref, out_ref):
    depth = left_ref.shape[1]

    @pl.loop(0, CHUNKS, unroll=2)
    def _(i):
        left = left_ref[chunk_rows(i), :]
        for j in range(GROUP):
            w = w_ref[j].reshape(LOCAL, depth)
            out_ref[pl.ds(i * 2, 2), :, j * LOCAL : (j + 1) * LOCAL] = (
                dot_nt(left, w).astype(BF).reshape(2, ROWS, LOCAL)
            )


def feed_forward(shard, tokens_ref, grads_ref, w_ref, down_ref, hid_ref, dgu_ref, j):
    odd = lax.rem(shard, 2)
    cols = slice(j * CHUNK, (j + 1) * CHUNK)
    late = slice(HID + j * CHUNK, HID + (j + 1) * CHUNK)

    @pl.loop(0, CHUNKS, unroll=2)
    def _(i):
        rows = chunk_rows(i)
        tokens, grads = token_chunk(tokens_ref, i), token_chunk(grads_ref, i)
        gate = dot(tokens, w_ref[:, :, :, :, cols].reshape(WIDTH, CHUNK))
        up = dot(tokens, w_ref[:, :, :, :, late].reshape(WIDTH, CHUNK))
        grad = dot_nt(grads, down_ref[cols, :])
        unit = lax.broadcasted_iota(jnp.int32, (CHUNK, CHUNK), 1) + (j * CHUNK - 64 * odd)
        mine = jnp.logical_and(unit >= 0, unit < LOCAL_FF)
        sigma = 1.0 / (1.0 + jnp.exp(-gate))
        silu = gate * sigma
        hid_ref[rows, cols] = jnp.where(mine, silu * up, 0.0).astype(BF)
        grad_gate = grad * up * (sigma * (1.0 + gate * (1.0 - sigma)))
        dgu_ref[rows, cols] = jnp.where(mine, grad_gate, 0.0).astype(BF)
        dgu_ref[rows, late] = jnp.where(mine, grad * silu, 0.0).astype(BF)


def outer(left_ref, right_ref, out_ref, first=0, last=None):
    depth = out_ref.shape[-1]
    size = 512 if depth % 512 == 0 else depth if depth < 512 else 256
    last = left_ref.shape[-1] // LOCAL if last is None else last

    @pl.loop(first, last, unroll=2)
    def _(m):
        cols = pl.ds(pl.multiple_of(m * LOCAL, LOCAL), LOCAL)
        if len(left_ref.shape) == 3:
            left = left_ref[:, :, cols].reshape(TOTAL, LOCAL)
        else:
            left = left_ref[:, cols]
        left = left.astype(F32).T.astype(BF)
        for j in range(depth // size):
            part = slice(j * size, (j + 1) * size)
            if len(right_ref.shape) == 3:
                right = right_ref[:, :, part].reshape(TOTAL, size)
            else:
                right = right_ref[:, part]
            out_ref[m, :, :, :, part] = dot(left, right).astype(BF).reshape(8, 2, SLAB, size)


class Return:
    def __init__(self, where, part, out, kind, own_sem, first_sends, first_recvs, sends, recvs):
        self.where, self.part, self.out, self.own_sem = where, part, out, own_sem
        self.first_sends, self.first_recvs = first_sends, first_recvs
        self.slabs = kind(where, out, sends, recvs)

    def first(self, n, offset, arriving=False):
        me = shard_at(self.where)
        source = shard_at(self.where, negative(offset)) if arriving else me
        return remote(
            self.part(shard_at(self.where, offset)),
            self.out.at[source, spot(self.where), self.where[4]],
            self.first_sends,
            self.first_recvs,
            n,
            device(self.where, offset),
        )

    def begin(self):
        for n, offset in enumerate(PEERS):
            self.first(n, offset).start()
        self.own().start()

    def own(self):
        me = shard_at(self.where)
        return pltpu.make_async_copy(
            self.part(me), self.out.at[me, spot(self.where), self.where[4]], self.own_sem
        )

    def middle(self):
        self.own().wait()
        for n, offset in enumerate(PEERS):
            self.first(n, offset, True).wait_recv()

    def turn(self, i):
        self.slabs.turn(i)

    def finish(self):
        self.slabs.finish()
        for n, offset in enumerate(PEERS):
            self.first(n, offset).wait_send()


class Vectors:
    ROUNDS = ((TWIN,), (NEAR,), ALONG)

    def __init__(self, where, msg, land, mine, round_land, first_sends, first_recvs, sends, recvs):
        self.where, self.msg, self.land, self.mine, self.round_land = where, msg, land, mine, round_land
        self.first_sends, self.first_recvs = first_sends, first_recvs
        self.sends, self.recvs = sends, recvs

    def first(self, n, offset, arriving=False):
        me = shard_at(self.where)
        source = shard_at(self.where, negative(offset)) if arriving else me
        return remote(
            self.msg.at[shard_at(self.where, offset)],
            self.land.at[source],
            self.first_sends,
            self.first_recvs,
            n,
            device(self.where, offset),
        )

    def begin(self):
        me = shard_at(self.where)
        for n, offset in enumerate(PEERS):
            self.first(n, offset).start()
        self.land[me] = self.msg[me]

    def middle(self):
        me = shard_at(self.where)
        for n, offset in enumerate(PEERS):
            self.first(n, offset, True).wait_recv()
        total = self.land[0]
        for source in range(1, GROUP):
            total = total + self.land[source]
        self.mine[0] = total
        for p in range(3):
            block = 3 * me + p
            self.mine[0, 4 + p : 5 + p, :] = self.land[lax.rem(block, GROUP), pl.ds(4 + block // GROUP, 1), :]

    def hop(self, n, i, step):
        return remote(self.mine.at[n], self.round_land.at[i], self.sends, self.recvs, i, device(self.where, step))

    def round(self, n):
        base = sum(len(r) for r in self.ROUNDS[:n])
        for i, step in enumerate(self.ROUNDS[n]):
            self.hop(n, base + i, step).start()
        total = self.mine[n]
        for i, step in enumerate(self.ROUNDS[n]):
            self.hop(n, base + i, step).wait_recv()
            total = total + self.round_land[base + i]
        self.mine[n + 1] = total

    def finish(self):
        for n, offset in enumerate(PEERS):
            self.first(n, offset).wait_send()
        for n, steps in enumerate(self.ROUNDS):
            base = sum(len(r) for r in self.ROUNDS[:n])
            for i, step in enumerate(steps):
                self.hop(n, base + i, step).wait_send()


VECTOR_SCRATCH = [
    pltpu.VMEM((GROUP, 8, LOCAL), F32),
    pltpu.VMEM((GROUP, 8, LOCAL), F32),
    pltpu.VMEM((4, 8, LOCAL), F32),
    pltpu.VMEM((5, 8, LOCAL), F32),
    DMA((7,)),
    DMA((7,)),
    DMA((5,)),
    DMA((5,)),
]


def params(cid=None, mib=56):
    if cid is None:
        return pltpu.CompilerParams(vmem_limit_bytes=mib * 2**20)
    return pltpu.CompilerParams(
        collective_id=cid, has_side_effects=True, vmem_limit_bytes=mib * 2**20
    )


class Copies:
    def __init__(self, sems):
        self.sems, self.flying = sems, {}

    def start(self, name, src, dst):
        copy = pltpu.make_async_copy(src, dst, self.sems.at[len(self.flying)])
        copy.start()
        self.flying[name] = [copy, False]

    def wait(self, *names):
        for name in names:
            entry = self.flying[name]
            if not entry[1]:
                entry[0].wait()
                entry[1] = True

    def finish(self):
        self.wait(*self.flying)


def front_kernel(
    x_ref, small_ref, table_ref, ow_ref, qkv_ref, gate_ref, up_ref, gy_ref,
    all_small, mid_ref, a1_out, a2_out, gy_out, wqkv_out, wgu_out, q_out, k_out, v_out, att_out, lse_out,
    a1, w_qkv, own_two, q, k, v, att, lse, vt, mixed, buf, land, local_sems, *sems,
):
    where = place()
    greet(where, PEERS + REP_NEIGHBOURS)
    me, rep = shard_at(where), rep_at(where)
    local = Copies(local_sems)

    def small(n, offset, arriving=False):
        owner = shard_at(where, negative(offset)) if arriving else me
        return remote(small_ref, all_small.at[owner], sems[0], sems[1], n, device(where, offset))

    for n, offset in enumerate(PEERS):
        small(n, offset).start()
    all_small[me] = small_ref[...]
    spread_qkv = Spread(where, qkv_cuts(qkv_ref, rep), w_qkv, *sems[2:7])
    spread_gu = Spread(where, gate_up_cuts(gate_ref, up_ref, rep), wgu_out, *sems[7:12])
    one = Gather(where, a1, *sems[12:14])
    two = Gather(where, a2_out, *sems[14:16], own=own_two)
    grads = Gather(where, gy_out, *sems[16:18], own=gy_ref)
    scatter = Scatter(where, buf, land, *sems[18:20])
    spread_qkv.begin()
    scaled, _ = standardize(x_ref[...].astype(F32))
    for n, offset in enumerate(PEERS):
        small(n, offset, True).wait_recv()
    a1[me] = (scaled * small_row(all_small, 0) + small_row(all_small, 1)).astype(BF)
    plan = Agenda()
    plan.add(agenda(one, TOKEN_TURNS, 0, 5))
    plan.until(1.0)
    spread_gu.begin()
    local.start("gy", gy_ref.at[0], gy_out.at[me])
    spread_qkv.middle()
    plan.add(slab_agenda(spread_qkv, 4, 4))
    plan.until(19)
    spread_gu.middle()
    plan.add(slab_agenda(spread_gu, 22, 8))
    plan.until(25)
    one.take_all()
    plan.add(agenda(grads, TOKEN_TURNS, 26, 5))
    plan.until(37)
    spread_qkv.slabs.take_all()
    local.start("a1", a1, a1_out)
    local.start("w_qkv", w_qkv, wqkv_out)
    for half in range(2):
        project(me, a1, w_qkv, all_small, table_ref, q, k, v, 2 * half, 2 * half + 2)
        plan.until(40 + 3 * half)
    attend(q, k, v, vt, mixed, att, lse, lambda i: plan.until(44 + 2 * i))
    for name, src, dst in (("q", q, q_out), ("k", k, k_out), ("v", v, v_out), ("att", att, att_out), ("lse", lse, lse_out)):
        local.start(name, src, dst)
    times(att, ow_ref, buf)
    plan.until(52)
    plan.add(agenda(scatter, TOKEN_TURNS, 53, 5, True))
    plan.until(80)
    scatter.take_all()
    mid = x_ref[...].astype(F32) + buf[me].astype(F32)
    mid_ref[...] = mid
    normed, _, _ = normalize(mid, small_row(all_small, 2), small_row(all_small, 3))
    own_two[0] = normed.astype(BF)
    plan.add(agenda(two, TOKEN_TURNS, 80, 5))
    plan.until(81)
    local.start("own_two", own_two.at[0], a2_out.at[me])
    plan.until(1000)
    spread_qkv.finish(True)
    for mover in (one, two, grads, scatter, spread_gu):
        mover.finish()
    for n, offset in enumerate(PEERS):
        small(n, offset).wait_send()
    local.finish()


def front(x, small, table, out_weight, qkv_weight, gate_weight, up_weight, gy):
    sds = jax.ShapeDtypeStruct
    tokens = sds((GROUP, ROWS, WIDTH), BF)
    head = sds((TOTAL, LOCAL), BF)
    token_sems = [DMA((COUNT,))] * 2
    return pl.pallas_call(
        front_kernel,
        out_shape=(
            sds((GROUP, 8, LOCAL), F32),
            sds((ROWS, WIDTH), F32),
            tokens,
            tokens,
            tokens,
            sds((GROUP, 8, 2, SLAB, 3 * LOCAL), BF),
            sds((GROUP, 8, 2, SLAB, 2 * HID), BF),
            head,
            head,
            head,
            head,
            sds((8, TOTAL), F32),
        ),
        in_specs=[VM] * 4 + [ANY] * 3 + [VM],
        out_specs=(VM, VM) + (ANY,) * 10,
        scratch_shapes=[
            pltpu.VMEM((GROUP, ROWS, WIDTH), BF),
            pltpu.VMEM((GROUP, 8, 2, SLAB, 3 * LOCAL), BF),
            pltpu.VMEM((1, ROWS, WIDTH), BF),
            *[pltpu.VMEM((TOTAL, LOCAL), BF)] * 4,
            pltpu.VMEM((8, TOTAL), F32),
            pltpu.VMEM((LOCAL, TOTAL), BF),
            pltpu.VMEM((LOCAL, TOTAL), F32),
            pltpu.VMEM((GROUP, ROWS, WIDTH), BF),
            pltpu.VMEM((LANDINGS, ROWS, FAR_COLS), BF),
            DMA((9,)),
            DMA((7,)),
            DMA((7,)),
        ]
        + spread_scratch(3)
        + spread_scratch(2)
        + token_sems * 4,
        compiler_params=params(0),
        name="front",
    )(x, small, table, out_weight, qkv_weight, gate_weight, up_weight, gy)


def middle_kernel(
    mid_ref, gy_own, small_ref, a2_in, gy_in, wgu_in, down_in,
    dmid_ref, sums_ref, dy_out, sgu_out, sdown_out, part_out,
    a2, gy, w, down, hid, dgu, buf, land, own, part, ggu, gdown, gu_0, gu_1, down_0, down_1, load_sems, local_sems, *sems,
):
    where = place()
    me, rep = shard_at(where), rep_at(where)
    odd = lax.rem(me, 2)
    loads = Copies(load_sems)

    def tile(j):
        for side in range(2):
            cols = pl.ds(side * HID + j * CHUNK, CHUNK)
            loads.start(("w", j, side), wgu_in.at[:, :, :, :, cols], w.at[:, :, :, :, cols])

    loads.start("a2", a2_in, a2)
    tile(0)
    loads.start("down", down_in, down.at[pl.ds(pl.multiple_of(64 * odd, 64), LOCAL_FF)])
    loads.start("gy", gy_in, gy)
    tile(1)
    tile(2)
    greet(where, NEIGHBOURS + REP_NEIGHBOURS)
    down[pl.ds(pl.multiple_of(LOCAL_FF * (1 - odd), 64), 64), :] = jnp.zeros((64, WIDTH), BF)
    loads.wait("a2", ("w", 0, 0), ("w", 0, 1), "down", "gy")
    for j in range(HID // CHUNK):
        if j:
            loads.wait(("w", j, 0), ("w", j, 1))
        feed_forward(me, a2, gy, w, down, hid, dgu, j)
    times_back(dgu, w, buf)
    scatter = Scatter(where, buf, land, *sems[0:2])
    gather = Gather(where, dy_out, *sems[2:4], own=own)
    local = Copies(local_sems)
    sum_gu = SlabScatter(where, ggu, gu_0, gu_1, *sems[4:6])
    sum_down = SlabScatter(where, gdown, down_0, down_1, *sems[6:8])
    plan = Agenda()
    plan.add(agenda(scatter, TOKEN_TURNS, 0, 5.5, True))
    plan.until(0.9)
    time = 0
    for m in range(GROUP):
        outer(a2, dgu, ggu, m, m + 1)
        time += 1.5
        plan.until(time)
    sum_gu.turn(0)
    for m in range(3):
        outer(hid, gy, gdown, m, m + 1)
        time += 2
        plan.until(time)
    sum_down.turn(0)
    plan.until(20)
    sum_gu.turn(1)
    plan.until(30)
    scatter.take_all()
    gain = small_row(small_ref, 2)
    _, scaled, inverse = normalize(mid_ref[...], gain, small_row(small_ref, 3))
    grad = buf[me].astype(F32)
    dmid = gy_own[0].astype(F32) + normalize_back(grad, gain, scaled, inverse)
    own[0] = dmid.astype(BF)
    plan.add(agenda(gather, TOKEN_TURNS, 32, 5.5))
    plan.until(34)
    local.start("own", own.at[0], dy_out.at[me])
    dmid_ref[...] = dmid
    sums_ref[0:1, :] = jnp.sum(grad * scaled, 0, keepdims=True)
    sums_ref[1:2, :] = jnp.sum(grad, 0, keepdims=True)
    sum_down.turn(1)
    plan.until(38)
    for n in range(CHUNKS):
        times(hid, down, part, n, n + 1)
        plan.until(40 + 2 * n)
    local.start("part", part, part_out)
    plan.until(54)
    sum_gu.turn(2)
    plan.until(56)
    sum_down.turn(2)
    plan.until(1000)
    gather.take_all()
    sum_gu.close()
    local.start("gu", sum_gu.total(), sgu_out)
    sum_down.close()
    local.start("down", sum_down.total(), sdown_out)
    for mover in (sum_gu, sum_down, gather, scatter, local):
        mover.finish()


def middle(mid, gy, small, a2, grads, w_gu, down_weight):
    sds = jax.ShapeDtypeStruct
    tokens = (GROUP, ROWS, WIDTH)
    return pl.pallas_call(
        middle_kernel,
        out_shape=(
            sds((ROWS, WIDTH), F32),
            sds((8, WIDTH), F32),
            sds(tokens, BF),
            sds((GROUP, SLAB, 2 * HID), BF),
            sds((3, SLAB, WIDTH), BF),
            sds(tokens, BF),
        ),
        in_specs=[VM] * 3 + [ANY] * 4,
        out_specs=(VM, VM) + (ANY,) * 4,
        scratch_shapes=[
            pltpu.VMEM(tokens, BF),
            pltpu.VMEM(tokens, BF),
            pltpu.VMEM((GROUP, 8, 2, SLAB, 2 * HID), BF),
            pltpu.VMEM((HID, WIDTH), BF),
            pltpu.VMEM((TOTAL, HID), BF),
            pltpu.VMEM((TOTAL, 2 * HID), BF),
            pltpu.VMEM(tokens, BF),
            pltpu.VMEM((LANDINGS, ROWS, FAR_COLS), BF),
            pltpu.VMEM((1, ROWS, WIDTH), BF),
            pltpu.VMEM(tokens, BF),
            pltpu.VMEM((GROUP, 8, 2, SLAB, 2 * HID), BF),
            pltpu.VMEM((3, 8, 2, SLAB, WIDTH), BF),
            *scatter_scratch(GROUP, 2 * HID),
            *scatter_scratch(3, WIDTH),
            DMA((9,)),
            DMA((4,)),
        ]
        + [DMA((COUNT,))] * 4
        + [DMA((SLAB_COUNT,))] * 4,
        compiler_params=params(1, 62),
        name="middle",
    )(mid, gy, small, a2, grads, w_gu, down_weight)


QKV_SPAN = (GROUP, 8, 2, SLAB, 3 * LOCAL)
HALF = 3 * LOCAL // 2
HALF_SPAN = (GROUP, 8, 2, SLAB, HALF)
GU_SPAN = (GROUP, 8, 2, SLAB, 2 * HID)
DOWN_SPAN = (3, 8, 2, SLAB, WIDTH)
OUT_SPAN = (4, 8, 2, SLAB, 512)


def back_kernel(
    x_ref, mid_ref, dmid_ref, small_ref, two_ref, table_ref, ow_ref,
    dy_in, a1_in, wqkv_in, q_in, k_in, v_in, att_in, lse_in, sgu_in, sdown_in, part_in,
    grad_ref, act_ref, vec_ref, gu_out, down_out, qkv_out, kv_out, out_out,
    toks, w, q, k, v, att, lse, da, kt, dqt, dk, dv, dqkv, buf, land,
    gqkv, gkv, gout, qkv_0, qkv_1, kv_0, kv_1, out_0, out_1, load_sems, own_sems, credit, *sems,
):
    where = place()
    me, rep = shard_at(where), rep_at(where)
    loads = Copies(load_sems)
    for name, src, dst in (
        ("part", part_in, buf), ("toks", dy_in, toks), ("q", q_in, q), ("k", k_in, k),
        ("v", v_in, v), ("lse", lse_in, lse), ("att", att_in, att), ("w", wqkv_in, w),
        ("down", sdown_in, down_out.at[:, spot(where), where[4]]),
    ):
        loads.start(name, src, dst)
    greet(where, PEERS + REP_NEIGHBOURS)
    down = Scatter(where, buf, land, *sems[0:2])
    one = Scatter(where, buf, land, *sems[2:4])
    sum_qkv = [
        SlabScatter(where, gqkv, qkv_0, qkv_1, *sems[4:6]),
        SlabScatter(where, gkv, kv_0, kv_1, *sems[28:30]),
    ]
    sum_out = SlabScatter(where, gout, out_0, out_1, *sems[6:8])
    back_gu = Return(where, lambda s: sgu_in.at[s], gu_out, RingGather, own_sems.at[0], *sems[8:12])
    back_qkv = [
        Return(
            where, lambda s: gqkv.at[s, spot(where), where[4]], qkv_out, SlabGather, own_sems.at[1], *sems[12:16]
        ),
        Return(
            where, lambda s: gkv.at[s, spot(where), where[4]], kv_out, SlabGather, own_sems.at[3], *sems[30:34]
        ),
    ]
    back_down = RingGather(where, down_out, *sems[16:18])
    back_out = RingGather(where, out_out, *sems[18:20])
    vectors = Vectors(where, *sems[20:28])
    plan = Agenda()
    back_gu.begin()
    loads.wait("part")
    plan.add(agenda(down, TOKEN_TURNS, 0, 6, True))
    plan.until(0.9)
    loads.wait("down")
    plan.add(slab_agenda(back_down, 1, 5))
    plan.until(1.5)
    loads.wait("toks")

    @pl.loop(0, CHUNKS, unroll=2)
    def _(i):
        da[chunk_rows(i), :] = dot_nt(token_chunk(toks, i), ow_ref[...]).astype(BF)

    back_gu.middle()
    plan.add(slab_agenda(back_gu, 5, 9))
    plan.until(5)
    loads.wait("q", "k", "v", "lse", "att")
    left = att[...].astype(F32).T.astype(BF)
    for n in range(4):
        right = toks[:, :, n * 512 : (n + 1) * 512].reshape(TOTAL, 512)
        gout[n] = dot(left, right).astype(BF).reshape(8, 2, SLAB, 512)
    loads.start("a1", a1_in, toks)
    plan.add([(7, sum_out, 0), (12, sum_out, 1), (30, sum_out, 2)])
    plan.until(7.5)
    attend_back(q, k, v, da, lse, kt, dqt, dk, dv, lambda i: plan.until(8.5 + 3 * i))
    plan.until(23)
    vectors.msg[...] = jnp.zeros_like(vectors.msg)
    for i in range(CHUNKS):
        rows = slice(i * CHUNK, (i + 1) * CHUNK)
        grad_q = dqt[:, rows].T * HEAD_DIM ** (-0.5)
        for j, value in enumerate((grad_q, dk[rows, :], dv[rows, :])):
            if j < 2:
                value = turned(value, table_ref, rows, -1)
            low = value.astype(BF)
            dqkv[rows, j * LOCAL : (j + 1) * LOCAL] = low
            vectors.msg[0, 4 + j : 5 + j, :] += jnp.sum(low.astype(F32), 0, keepdims=True)
    plan.until(25)
    loads.wait("a1", "w")
    outer(toks, dqkv.at[:, pl.ds(0, HALF)], gqkv)
    sum_qkv[0].turn(0)
    plan.until(29)
    outer(toks, dqkv.at[:, pl.ds(HALF, HALF)], gkv)
    sum_qkv[1].turn(0)
    plan.until(32)
    sum_qkv[0].turn(1)
    down.finish()
    for step in NEIGHBOURS:
        pl.semaphore_signal(credit, inc=1, device_id=device(where, step), device_id_type=MESH)
    act_ref[...] = (mid_ref[...] + buf[me].astype(F32)).astype(BF)
    times_back(dqkv, w, buf)
    sum_qkv[1].turn(1)
    pl.semaphore_wait(credit, len(NEIGHBOURS))
    plan.add(agenda(one, TOKEN_TURNS, 38, 5.5, True))
    plan.until(40)
    sum_out.close()
    out_own = pltpu.make_async_copy(
        sum_out.total(), out_out.at[:, spot(where), where[4]], own_sems.at[2]
    )
    out_own.start()
    plan.until(44)
    sum_qkv[0].turn(2)
    out_own.wait()
    plan.add(slab_agenda(back_out, 44, 4))
    plan.until(50)
    sum_qkv[0].close()
    back_qkv[0].begin()
    sum_qkv[1].turn(2)
    plan.until(53)
    back_qkv[0].middle()
    back_qkv[0].turn(0)
    plan.until(55)
    sum_qkv[1].close()
    back_qkv[1].begin()
    back_qkv[0].turn(1)
    plan.until(58)
    back_qkv[1].middle()
    back_qkv[1].turn(0)
    plan.until(62)
    one.take_all()
    gain = small_row(small_ref, 0)
    _, scaled, inverse = normalize(x_ref[...].astype(F32), gain, small_row(small_ref, 1))
    grad = buf[me].astype(F32)
    first, second = jnp.sum(grad * scaled, 0, keepdims=True), jnp.sum(grad, 0, keepdims=True)
    for d in range(GROUP):
        cols = slice(d * LOCAL, (d + 1) * LOCAL)
        vectors.msg[d, 0:1, :] = first[:, cols]
        vectors.msg[d, 1:2, :] = second[:, cols]
        vectors.msg[d, 2:4, :] = two_ref[0:2, cols]
        if d:
            vectors.msg[d, 4:7, :] = vectors.msg[0, 4:7, :]
    vectors.begin()
    back_qkv[1].turn(1)
    back_qkv[0].turn(2)
    grad_ref[...] = dmid_ref[...] + normalize_back(grad, gain, scaled, inverse)
    vectors.middle()
    vectors.round(0)
    vectors.round(1)
    vectors.round(2)
    vec_ref[...] = vectors.mine[3]
    plan.until(1000)
    back_qkv[1].turn(2)
    for mover in (one, *sum_qkv, sum_out, back_gu, back_down, back_out, *back_qkv, vectors):
        mover.finish()
    loads.finish()


def back(x, mid, dmid, small, sums_two, table, out_weight, dy, a1, w_qkv, q, k, v, att, lse, s_gu, s_down, part_down):
    sds = jax.ShapeDtypeStruct
    tokens = (GROUP, ROWS, WIDTH)
    slab_sems = [DMA((SLAB_COUNT,))] * 2
    return pl.pallas_call(
        back_kernel,
        out_shape=(
            sds((ROWS, WIDTH), F32),
            sds((ROWS, WIDTH), BF),
            sds((8, LOCAL), F32),
            *[sds(s, BF) for s in (GU_SPAN, DOWN_SPAN, HALF_SPAN, HALF_SPAN, OUT_SPAN)],
        ),
        in_specs=[VM] * 7 + [ANY] * 11,
        out_specs=(VM,) * 3 + (ANY,) * 5,
        scratch_shapes=[
            pltpu.VMEM(tokens, BF),
            pltpu.VMEM(QKV_SPAN, BF),
            *[pltpu.VMEM((TOTAL, LOCAL), BF)] * 4,
            pltpu.VMEM((8, TOTAL), F32),
            pltpu.VMEM((TOTAL, LOCAL), BF),
            pltpu.VMEM((LOCAL, TOTAL), BF),
            pltpu.VMEM((LOCAL, TOTAL), F32),
            pltpu.VMEM((TOTAL, LOCAL), F32),
            pltpu.VMEM((TOTAL, LOCAL), F32),
            pltpu.VMEM((TOTAL, 3 * LOCAL), BF),
            pltpu.VMEM(tokens, BF),
            pltpu.VMEM((LANDINGS, ROWS, FAR_COLS), BF),
            pltpu.VMEM(HALF_SPAN, BF),
            pltpu.VMEM(HALF_SPAN, BF),
            pltpu.VMEM(OUT_SPAN, BF),
            *scatter_scratch(GROUP, HALF),
            *scatter_scratch(GROUP, HALF),
            *scatter_scratch(4, 512),
            DMA((10,)),
            DMA((4,)),
            pltpu.SemaphoreType.REGULAR,
        ]
        + [DMA((COUNT,))] * 4
        + slab_sems * 2
        + ([DMA((7,))] * 2 + slab_sems) * 2
        + slab_sems * 2
        + VECTOR_SCRATCH
        + slab_sems
        + [DMA((7,))] * 2
        + slab_sems,
        compiler_params=params(2, 60),
        name="back",
    )(x, mid, dmid, small, sums_two, table, out_weight, dy, a1, w_qkv, q, k, v, att, lse, s_gu, s_down, part_down)


def unpack_kernel(odd_ref, gu_ref, qkv_ref, kv_ref, out_ref, down_ref, gate_out, up_out, qkv_out, out_out, down_out):
    for side, ref in enumerate((gate_out, up_out)):
        cols = slice(side * HID, (side + 1) * HID)
        for t in range(GROUP // 2):
            left, right = gu_ref[2 * t, :, cols].astype(F32), gu_ref[2 * t + 1, :, cols].astype(F32)
            ref[:, t * 2 * LOCAL_FF : (t + 1) * 2 * LOCAL_FF] = jnp.concatenate(
                [left[:, :640], left[:, 640:] + right[:, :128], right[:, 128:]], axis=1
            )
    for s in range(GROUP):
        for j in range(3):
            for part in range(2):
                cols = j * LOCAL + part * 128
                ref, at = (qkv_ref, cols) if cols < HALF else (kv_ref, cols - HALF)
                first = j * WIDTH + s * LOCAL + part * 128
                qkv_out[:, first : first + 128] = ref[s, :, at : at + 128].astype(F32)
    for n in range(4):
        out_out[:, n * 512 : (n + 1) * 512] = out_ref[n].astype(F32)
    rows = LOCAL_FF // 4
    first = pl.multiple_of(64 * odd_ref[0] + rows * pl.program_id(0), SLAB)
    down_out[...] = down_ref[pl.ds(first, rows), :].astype(F32)


def unpack(odd, g_gu, g_qkv, g_kv, g_out, g_down):
    sds = jax.ShapeDtypeStruct
    rows = LOCAL // 4
    return pl.pallas_call(
        unpack_kernel,
        grid_spec=pltpu.PrefetchScalarGridSpec(
            num_scalar_prefetch=1,
            grid=(4,),
            in_specs=[
                pl.BlockSpec((GROUP, rows, 2 * HID), lambda r, _: (0, r, 0)),
                *[pl.BlockSpec((GROUP, rows, HALF), lambda r, _: (0, r, 0))] * 2,
                pl.BlockSpec((4, rows, 512), lambda r, _: (0, r, 0)),
                pl.BlockSpec((HID, WIDTH), lambda r, _: (0, 0)),
            ],
            out_specs=[
                pl.BlockSpec((rows, FF), lambda r, _: (r, 0)),
                pl.BlockSpec((rows, FF), lambda r, _: (r, 0)),
                pl.BlockSpec((rows, 3 * WIDTH), lambda r, _: (r, 0)),
                pl.BlockSpec((rows, WIDTH), lambda r, _: (r, 0)),
                pl.BlockSpec((LOCAL_FF // 4, WIDTH), lambda r, _: (r, 0)),
            ],
        ),
        out_shape=(
            sds((LOCAL, FF), F32),
            sds((LOCAL, FF), F32),
            sds((LOCAL, 3 * WIDTH), F32),
            sds((LOCAL, WIDTH), F32),
            sds((LOCAL_FF, WIDTH), F32),
        ),
        compiler_params=params(),
        name="unpack",
    )(odd.reshape(1), g_gu, g_qkv, g_kv, g_out, g_down)


def shards(
    inputs,
    cotangent,
    ln1_gain,
    ln1_bias,
    qkv_weight,
    qkv_bias,
    out_weight,
    ln2_gain,
    ln2_bias,
    gate_weight,
    up_weight,
    down_weight,
):
    batch, length, width = inputs.shape
    odd = lax.rem(lax.axis_index("shard"), 2)
    table = jnp.asarray(rotary_tables())
    x = inputs.reshape(length, width)
    small, at = jnp.zeros((8 * LOCAL,), F32), 0
    for vector in (ln1_gain, ln1_bias, ln2_gain, ln2_bias, qkv_bias):
        small += jnp.pad(vector.astype(F32), (at, 8 * LOCAL - at - vector.shape[0]))
        at += vector.shape[0]
    small = small.reshape(8, LOCAL)
    all_small, mid, a1, a2, grads, w_qkv, w_gu, q, k, v, att, lse = front(
        x, small, table, out_weight, qkv_weight, gate_weight, up_weight, cotangent
    )
    dmid, sums_two, dy, s_gu, s_down, part_down = middle(
        mid, cotangent, all_small, a2, grads, w_gu, down_weight
    )
    input_grad, activations, vectors, g_gu, g_down, g_qkv, g_kv, g_out = back(
        x, mid, dmid, all_small, sums_two, table, out_weight, dy, a1, w_qkv, q, k, v, att, lse, s_gu, s_down, part_down
    )
    g_gate, g_up, g_qkv, g_out, g_down = unpack(
        odd,
        g_gu.reshape(GROUP, LOCAL, 2 * HID),
        g_qkv.reshape(GROUP, LOCAL, HALF),
        g_kv.reshape(GROUP, LOCAL, HALF),
        g_out.reshape(4, LOCAL, 512),
        g_down.reshape(HID, width),
    )
    return (
        activations.reshape(batch, length, width),
        input_grad.reshape(batch, length, width),
        vectors[0],
        vectors[1],
        g_qkv,
        vectors[4:7].reshape(3 * LOCAL),
        g_out,
        vectors[2],
        vectors[3],
        g_gate,
        g_up,
        g_down,
    )


def solution(mesh):
    tokens, vector, matrix = P("rep", "shard", None), P("shard"), P("shard", None)
    return jax.shard_map(
        shards,
        mesh=mesh,
        in_specs=(tokens, tokens, vector, vector, matrix, vector, matrix, vector, vector, matrix, matrix, matrix),
        out_specs=(tokens, tokens, vector, vector, matrix, vector, matrix, vector, vector, matrix, matrix, matrix),
        check_vma=False,
    )
```

time: 599 us -> 408 us (0.68)
  the two profiles are of different devices: /device:TPU:8 before, /device:TPU:3 now
where the time goes in v2:
time: 408 us; the launch traced here: 401 us
  Pallas kernels  394 us (97%)
  local copies, waits for them, and re-layouts  5.1 us (1%)
    pallas_call x1, Pallas kernels, back(): pl.pallas_call(back_kernel, out_shape=(sds((ROWS, WIDTH), F32), sds((ROWS...  136 us
    pallas_call x1, Pallas kernels, front(): pl.pallas_call(front_kernel, out_shape=(sds((GROUP, 8, LOCAL), F32), sds(...  136 us
    pallas_call x1, Pallas kernels, middle(): pl.pallas_call(middle_kernel, out_shape=(sds((ROWS, WIDTH), F32), sds((8,...  109 us
    pallas_call x1, Pallas kernels, unpack(): pl.pallas_call(unpack_kernel, grid_spec=pltpu.PrefetchScalarGridSpec(num_...  12.9 us

profile of v2, /device:TPU:3, one launch (start us, length us, event | category | flops | bytes accessed | tf_op | source)
XLA Modules:
  0.0 400.8 jit_solution(14128415085605735657)
XLA Ops:
  0.7 0.7 convert_add_fusion
  1.4 0.6 reshape.58.small_ref
  2.0 135.8 %front.1 = (f32[8,8,256]{2,1,0:T(8,128)}, f32[128,2048]{1,0:T(8,128)}, bf16[8,128,2048]{2,1,0:T(8,128)(2,1)}, bf16[8,128,2048]{2,1,0:T(8,128)(2,1)}, bf16[8,128,...) custom-call(bf16[128,2048]{1,0:T(8,128)(2,1)} %bitcast.15, ...), custom_call_target="tpu_custom_call" | custom-call | tf_op jit(solution)/shard_map/front/pallas_call | solution.py:998
  137.8 109.1 %middle.1 = (f32[128,2048]{1,0:T(8,128)}, f32[8,2048]{1,0:T(8,128)}, bf16[8,128,2048]{2,1,0:T(8,128)(2,1)}, bf16[8,16,1536]{2,1,0:T(8,128)(2,1)}, bf16[3,16,2048...) custom-call(f32[128,2048]{1,0:T(8,128)} %get-tuple-element.43.mid_ref, bf16[1,128,2048]{2,1,0:T(8,128)(2,1)} %gy_own.1, ...), custom_call_target="tpu_custom_call" | custom-call | tf_op jit(solution)/shard_map/middle/pallas_call | solution.py:1124
  246.9 136.0 %back.1 = (f32[128,2048]{1,0:T(8,128)}, bf16[128,2048]{1,0:T(8,128)(2,1)}, f32[8,256]{1,0:T(8,128)}, bf16[8,8,2,16,1536]{4,3,2,1,0:T(8,128)(2,1)}, bf16[3,8,2,16...) custom-call(bf16[128,2048]{1,0:T(8,128)(2,1)} %bitcast.16, ...), custom_call_target="tpu_custom_call" | custom-call | tf_op jit(solution)/shard_map/back/pallas_call | solution.py:1316
  382.9 0.7 slice.17
  383.6 1.4 fusion
  385.0 0.6 reshape.67
  385.6 0.0 copy-start.1
  385.6 0.0 copy-start
  385.6 12.9 %unpack.1 = (f32[256,5632]{1,0:T(8,128)}, f32[256,5632]{1,0:T(8,128)}, f32[256,6144]{1,0:T(8,128)}, f32[256,2048]{1,0:T(8,128)}, f32[704,2048]{1,0:T(8,128)}) custom-call(s32[1]{0:T(128)} %bitcast.5.odd_ref, bf16[8,256,1536]{2,1,0:T(8,128)(2,1)} %bitcast.13, bf16[8,256,384]{2,1,0:T(8,128)(2,1)} %bitcast.17, bf16[8,256,384]{2,1,0:T(8,128)(2,1)} %bitcast.18, ...), custom_call_target="tpu_custom_call" | custom-call | tf_op jit(solution)/shard_map/unpack/pallas_call | solution.py:1387
  398.5 0.0 copy-done.1
  398.5 0.8 copy.27
  399.3 0.0 copy-done
  399.3 1.0 copy.28
Async XLA Ops:
  385.6 12.9 %copy-start.1 = (bf16[128,2048]{1,0:T(8,128)(2,1)S(1)}, bf16[128,2048]{1,0:T(8,128)(2,1)}, u32[]{:S(2)}) copy-start(bf16[128,2048]{1,0:T(8,128)(2,1)} %get-tuple-element.61) | copy-start | bytes 1572868
  385.6 13.7 %copy-start = (f32[128,2048]{1,0:T(8,128)S(1)}, f32[128,2048]{1,0:T(8,128)}, u32[]{:S(2)}) copy-start(f32[128,2048]{1,0:T(8,128)} %get-tuple-element.62) | copy-start | bytes 3145732

commit v3 on v2

--- a/solution.py
+++ b/solution.py
@@ -106,37 +106,38 @@
 def token_moves():
     moves = []
 
-    def add(owner, part, step, first, turn):
-        moves.append((owner, part, step, first, turn))
+    def add(owner, part, step, first, turn, back):
+        moves.append((owner, part, step, first, turn, back))
         return len(moves) - 1
 
     near, far = (0, NEAR_COLS), (NEAR_COLS, FAR_COLS)
     whole, top, low = (0, ROWS), (0, ROWS // 2), (ROWS // 2, ROWS // 2)
     up2 = (0, 2, 0, 0, 0)
-    up = add(HERE, (whole, near), UP, None, 0)
-    down = add(HERE, (whole, near), DOWN, None, 0)
-    add(HERE, (whole, near), FAR, None, 0.2)
-    a = add(DOWN, (top, near), UP, up, 1)
-    b = add(UP, (low, near), DOWN, down, 1)
-    add(DOWN, (whole, near), FAR, up, 1.1)
-    add(UP, (whole, near), FAR, down, 1.1)
-    add(up2, (top, near), FAR, a, 2)
-    add(up2, (low, near), FAR, b, 2)
-    over = add(HERE, (whole, far), FAR, None, 0.1)
-    up = add(HERE, (whole, far), UP, None, 1.1)
-    down = add(HERE, (whole, far), DOWN, None, 1.1)
-    add(DOWN, (top, far), UP, up, 3)
-    add(UP, (low, far), DOWN, down, 3)
-    up = add(FAR, (whole, far), UP, over, 2.5)
-    down = add(FAR, (whole, far), DOWN, over, 2.5)
-    add(tuple(p + q for p, q in zip(FAR, DOWN)), (top, far), UP, up, 4)
-    add(tuple(p + q for p, q in zip(FAR, UP)), (low, far), DOWN, down, 4)
+    up = add(HERE, (whole, near), UP, None, 0, 15.5)
+    down = add(HERE, (whole, near), DOWN, None, 0, 15.5)
+    add(HERE, (whole, near), FAR, None, 0.2, 0.3)
+    a = add(DOWN, (top, near), UP, up, 5.5, 7)
+    b = add(UP, (low, near), DOWN, down, 5.5, 7)
+    add(DOWN, (whole, near), FAR, up, 5.6, 0.2)
+    add(UP, (whole, near), FAR, down, 5.6, 0.2)
+    add(up2, (top, near), FAR, a, 10, 0)
+    add(up2, (low, near), FAR, b, 10, 0)
+    over = add(HERE, (whole, far), FAR, None, 0.1, 15)
+    up = add(HERE, (whole, far), UP, None, 0.3, 9)
+    down = add(HERE, (whole, far), DOWN, None, 0.3, 9)
+    add(DOWN, (top, far), UP, up, 13, 0.1)
+    add(UP, (low, far), DOWN, down, 13, 0.1)
+    up = add(FAR, (whole, far), UP, over, 11.5, 6)
+    down = add(FAR, (whole, far), DOWN, over, 11.5, 6)
+    add(tuple(p + q for p, q in zip(FAR, DOWN)), (top, far), UP, up, 19.5, 0)
+    add(tuple(p + q for p, q in zip(FAR, UP)), (low, far), DOWN, down, 19.5, 0)
     return tuple(moves)
 
 
 MOVES = token_moves()
 COUNT = len(MOVES)
 TURNS = tuple(sorted(range(COUNT), key=lambda i: MOVES[i][4]))
+BACK_TURNS = tuple(sorted(range(COUNT), key=lambda i: MOVES[i][5]))
 FED = tuple(tuple(j for j in range(COUNT) if MOVES[j][3] == i) for i in range(COUNT))
 NEIGHBOURS = (FAR, UP, DOWN)
 LANDS = {}
@@ -157,7 +158,7 @@
         self.got = set()
 
     def move(self, i, arriving=False):
-        owner, part, step, _, _ = MOVES[i]
+        owner, part, step = MOVES[i][:3]
         block = shard_at(self.where, less(owner, step) if arriving else owner)
         ref = token_part(self.ref, block, part)
         src = ref
@@ -179,11 +180,13 @@
         for i in TURNS:
             self.take(i)
 
-    def finish(self):
-        for i in TURNS:
-            self.take(i)
+    def settle(self):
         for i in TURNS:
             self.move(i).wait_send()
+
+    def finish(self):
+        self.take_all()
+        self.settle()
 
     def run(self):
         for i in TURNS:
@@ -191,11 +194,9 @@
         self.finish()
 
 
-def agenda(mover, turns, start, unit, backwards=False):
-    last = max(turns[i] for i in turns)
-    return [
-        (start + unit * ((last - t) if backwards else t), mover, i) for i, t in turns.items()
-    ]
+def agenda(mover, start):
+    column = 5 if isinstance(mover, Scatter) else 4
+    return [(start + MOVES[i][column], mover, i) for i in range(COUNT)]
 
 
 def slab_agenda(mover, start, unit):
@@ -216,16 +217,13 @@
             mover.turn(i)
 
 
-TOKEN_TURNS = {i: MOVES[i][4] for i in range(COUNT)}
-
-
 class Scatter:
     def __init__(self, where, buf, land, sends, recvs):
         self.where, self.buf, self.land, self.sends, self.recvs = where, buf, land, sends, recvs
         self.got = set()
 
     def move(self, i, arriving=False):
-        owner, part, step, _, _ = MOVES[i]
+        owner, part, step = MOVES[i][:3]
         block = shard_at(self.where, owner if arriving else less(owner, step))
         (row, rows), (col, cols) = part
         return remote(
@@ -241,7 +239,7 @@
         if i in self.got:
             return
         self.got.add(i)
-        owner, ((row, rows), (col, cols)), _, _, _ = MOVES[i]
+        owner, ((row, rows), (col, cols)) = MOVES[i][:2]
         self.move(i, True).wait_recv()
         at = (shard_at(self.where, owner), pl.ds(row, rows), pl.ds(col, cols))
         total = self.buf[at].astype(F32) + self.land[LANDS[i], pl.ds(row, rows), pl.ds(0, cols)].astype(F32)
@@ -253,17 +251,19 @@
         self.move(i).start()
 
     def take_all(self):
-        for i in reversed(TURNS):
+        for i in BACK_TURNS:
             self.take(i)
 
+    def settle(self):
+        for i in BACK_TURNS:
+            self.move(i).wait_send()
+
     def finish(self):
-        for i in reversed(TURNS):
-            self.take(i)
-        for i in reversed(TURNS):
-            self.move(i).wait_send()
+        self.take_all()
+        self.settle()
 
     def run(self):
-        for i in reversed(TURNS):
+        for i in BACK_TURNS:
             self.turn(i)
         self.finish()
 
@@ -518,6 +518,103 @@
 
     def total(self):
         return self.ref.at[:, spot(self.where), self.where[4]]
+
+
+class RingScatter:
+    NORTH, SOUTH, ACROSS = ALONG
+    HOPS = (
+        (TWIN, HERE, 2),
+        (NORTH, NEAR, 1),
+        (SOUTH, NEAR, 1),
+        (NORTH, HERE, 1),
+        (SOUTH, HERE, 1),
+        (NORTH, NEAR, 0),
+        (SOUTH, NEAR, 0),
+        (NORTH, HERE, 0),
+        (SOUTH, HERE, 0),
+        (NEAR, HERE, 0),
+    )
+
+    def __init__(self, where, ref, twin, land, sends, recvs):
+        self.where, self.ref, self.twin, self.land = where, ref, twin, land
+        self.sends, self.recvs = sends, recvs
+        self.done = 0
+        self.cut = ref.shape[0] - ref.shape[0] // 2
+
+    def blocks(self, i):
+        step, _, kind = self.HOPS[i]
+        size = self.ref.shape[0]
+        if kind != 1:
+            return 0, size
+        return (0, self.cut) if step == self.NORTH else (self.cut, size)
+
+    def hop(self, i, arriving=False):
+        (step, base, kind), core = self.HOPS[i], self.where[4]
+        if kind == 2:
+            src, dst = self.ref.at[:, :, 1 - core], self.twin
+        else:
+            owner = both(base, self.ACROSS if kind else step)
+            first, last = self.blocks(i)
+            span = pl.ds(first, last - first)
+            src, dst = self.ref.at[span, spot(self.where, owner), core], self.land.at[i - 1, span]
+        return remote(src, dst, self.sends, self.recvs, i, device(self.where, step))
+
+    def add(self, i, base):
+        step, _, kind = self.HOPS[i]
+        core = self.where[4]
+        self.hop(i, True).wait_recv()
+        at = spot(self.where, both(base, step) if kind else base)
+        first, last = self.blocks(i)
+
+        @pl.loop(first, last)
+        def _(n):
+            total = self.ref[n, at, core].astype(F32) + self.land[i - 1, n].astype(F32)
+            self.ref[n, at, core] = total.astype(BF)
+
+    def turn(self, stage):
+        assert stage == self.done
+        self.done += 1
+        core = self.where[4]
+        if stage == 0:
+            starts = (0,)
+        elif stage == 1:
+            self.hop(0, True).wait_recv()
+
+            @pl.loop(0, self.ref.shape[0])
+            def _(n):
+                total = self.ref[n, :, core].astype(F32) + self.twin[n].astype(F32)
+                self.ref[n, :, core] = total.astype(BF)
+
+            starts = (1, 2, 3, 4)
+        elif stage == 2:
+            self.add(1, NEAR)
+            self.add(2, NEAR)
+            starts = (5, 6)
+        elif stage == 3:
+            self.add(3, HERE)
+            self.add(4, HERE)
+            starts = (7, 8)
+        else:
+            self.add(5, NEAR)
+            self.add(6, NEAR)
+            starts = (9,)
+        for i in starts:
+            self.hop(i).start()
+
+    def close(self):
+        for i in (7, 8, 9):
+            self.add(i, HERE)
+
+    def finish(self):
+        for i in range(10):
+            self.hop(i).wait_send()
+
+    def total(self):
+        return self.ref.at[:, spot(self.where), self.where[4]]
+
+
+def ring_scratch(n, cols):
+    return [pltpu.VMEM((n, 8, SLAB, cols), BF), pltpu.VMEM((9, n, SLAB, cols), BF)]
 
 
 def scatter_scratch(n, cols):
@@ -947,7 +1044,7 @@
         small(n, offset, True).wait_recv()
     a1[me] = (scaled * small_row(all_small, 0) + small_row(all_small, 1)).astype(BF)
     plan = Agenda()
-    plan.add(agenda(one, TOKEN_TURNS, 0, 5))
+    plan.add(agenda(one, 0))
     plan.until(1.0)
     spread_gu.begin()
     local.start("gy", gy_ref.at[0], gy_out.at[me])
@@ -958,7 +1055,7 @@
     plan.add(slab_agenda(spread_gu, 22, 8))
     plan.until(25)
     one.take_all()
-    plan.add(agenda(grads, TOKEN_TURNS, 26, 5))
+    plan.add(agenda(grads, 26))
     plan.until(37)
     spread_qkv.slabs.take_all()
     local.start("a1", a1, a1_out)
@@ -971,14 +1068,14 @@
         local.start(name, src, dst)
     times(att, ow_ref, buf)
     plan.until(52)
-    plan.add(agenda(scatter, TOKEN_TURNS, 53, 5, True))
+    plan.add(agenda(scatter, 53))
     plan.until(80)
     scatter.take_all()
     mid = x_ref[...].astype(F32) + buf[me].astype(F32)
     mid_ref[...] = mid
     normed, _, _ = normalize(mid, small_row(all_small, 2), small_row(all_small, 3))
     own_two[0] = normed.astype(BF)
-    plan.add(agenda(two, TOKEN_TURNS, 80, 5))
+    plan.add(agenda(two, 80))
     plan.until(81)
     local.start("own_two", own_two.at[0], a2_out.at[me])
     plan.until(1000)
@@ -1038,7 +1135,7 @@
 def middle_kernel(
     mid_ref, gy_own, small_ref, a2_in, gy_in, wgu_in, down_in,
     dmid_ref, sums_ref, dy_out, sgu_out, sdown_out, part_out,
-    a2, gy, w, down, hid, dgu, buf, land, own, part, ggu, gdown, gu_0, gu_1, down_0, down_1, load_sems, local_sems, *sems,
+    a2, gy, w, down, hid, dgu, buf, land, own, part, ggu, gdown, one_0, one_1, two_0, two_1, down_0, down_1, load_sems, local_sems, *sems,
 ):
     where = place()
     me, rep = shard_at(where), rep_at(where)
@@ -1067,24 +1164,29 @@
     scatter = Scatter(where, buf, land, *sems[0:2])
     gather = Gather(where, dy_out, *sems[2:4], own=own)
     local = Copies(local_sems)
-    sum_gu = SlabScatter(where, ggu, gu_0, gu_1, *sems[4:6])
-    sum_down = SlabScatter(where, gdown, down_0, down_1, *sems[6:8])
+    half = GROUP // 2
+    sum_gu = [
+        RingScatter(where, ggu.at[pl.ds(0, half)], one_0, one_1, *sems[4:6]),
+        RingScatter(where, ggu.at[pl.ds(half, half)], two_0, two_1, *sems[8:10]),
+    ]
+    sum_down = RingScatter(where, gdown, down_0, down_1, *sems[6:8])
     plan = Agenda()
-    plan.add(agenda(scatter, TOKEN_TURNS, 0, 5.5, True))
+    plan.add(agenda(scatter, 0))
     plan.until(0.9)
     time = 0
     for m in range(GROUP):
         outer(a2, dgu, ggu, m, m + 1)
-        time += 1.5
+        time += 1.4
         plan.until(time)
-    sum_gu.turn(0)
+        if m == half - 1:
+            plan.add([(6, sum_gu[0], 0), (10.5, sum_gu[0], 1), (15, sum_gu[0], 2), (20, sum_gu[0], 3), (25, sum_gu[0], 4)])
+    plan.add([(11.3, sum_gu[1], 0), (15.5, sum_gu[1], 1), (23, sum_gu[1], 2), (29, sum_gu[1], 3), (36, sum_gu[1], 4)])
+    plan.until(time)
     for m in range(3):
         outer(hid, gy, gdown, m, m + 1)
         time += 2
         plan.until(time)
-    sum_down.turn(0)
-    plan.until(20)
-    sum_gu.turn(1)
+    plan.add([(17.5, sum_down, 0), (22, sum_down, 1), (33.5, sum_down, 2), (37, sum_down, 3), (42, sum_down, 4)])
     plan.until(30)
     scatter.take_all()
     gain = small_row(small_ref, 2)
@@ -1092,29 +1194,26 @@
     grad = buf[me].astype(F32)
     dmid = gy_own[0].astype(F32) + normalize_back(grad, gain, scaled, inverse)
     own[0] = dmid.astype(BF)
-    plan.add(agenda(gather, TOKEN_TURNS, 32, 5.5))
-    plan.until(34)
+    plan.add(agenda(gather, 32))
+    plan.until(33)
     local.start("own", own.at[0], dy_out.at[me])
     dmid_ref[...] = dmid
     sums_ref[0:1, :] = jnp.sum(grad * scaled, 0, keepdims=True)
     sums_ref[1:2, :] = jnp.sum(grad, 0, keepdims=True)
-    sum_down.turn(1)
-    plan.until(38)
+    plan.until(37)
     for n in range(CHUNKS):
         times(hid, down, part, n, n + 1)
-        plan.until(40 + 2 * n)
+        plan.until(39 + 2 * n)
     local.start("part", part, part_out)
-    plan.until(54)
-    sum_gu.turn(2)
-    plan.until(56)
-    sum_down.turn(2)
+    plan.until(50)
+    for n in range(2):
+        sum_gu[n].close()
+        local.start(("gu", n), sum_gu[n].total(), sgu_out.at[pl.ds(half * n, half)])
     plan.until(1000)
-    gather.take_all()
-    sum_gu.close()
-    local.start("gu", sum_gu.total(), sgu_out)
     sum_down.close()
     local.start("down", sum_down.total(), sdown_out)
-    for mover in (sum_gu, sum_down, gather, scatter, local):
+    gather.take_all()
+    for mover in (*sum_gu, sum_down, gather, scatter, local):
         mover.finish()
 
 
@@ -1146,13 +1245,14 @@
             pltpu.VMEM(tokens, BF),
             pltpu.VMEM((GROUP, 8, 2, SLAB, 2 * HID), BF),
             pltpu.VMEM((3, 8, 2, SLAB, WIDTH), BF),
-            *scatter_scratch(GROUP, 2 * HID),
-            *scatter_scratch(3, WIDTH),
+            *ring_scratch(GROUP // 2, 2 * HID),
+            *ring_scratch(GROUP // 2, 2 * HID),
+            *ring_scratch(3, WIDTH),
             DMA((9,)),
-            DMA((4,)),
+            DMA((5,)),
         ]
         + [DMA((COUNT,))] * 4
-        + [DMA((SLAB_COUNT,))] * 4,
+        + [DMA((SLAB_COUNT,))] * 6,
         compiler_params=params(1, 62),
         name="middle",
     )(mid, gy, small, a2, grads, w_gu, down_weight)
@@ -1170,20 +1270,21 @@
     x_ref, mid_ref, dmid_ref, small_ref, two_ref, table_ref, ow_ref,
     dy_in, a1_in, wqkv_in, q_in, k_in, v_in, att_in, lse_in, sgu_in, sdown_in, part_in,
     grad_ref, act_ref, vec_ref, gu_out, down_out, qkv_out, kv_out, out_out,
-    toks, w, q, k, v, att, lse, da, kt, dqt, dk, dv, dqkv, buf, land,
-    gqkv, gkv, gout, qkv_0, qkv_1, kv_0, kv_1, out_0, out_1, load_sems, own_sems, credit, *sems,
+    toks, a1, w, q, k, v, att, lse, da, kt, dqt, dk, dv, dqkv, buf, land, buf_down, land_down,
+    gqkv, gkv, gout, qkv_0, qkv_1, kv_0, kv_1, out_0, out_1, load_sems, own_sems, *sems,
 ):
     where = place()
     me, rep = shard_at(where), rep_at(where)
     loads = Copies(load_sems)
     for name, src, dst in (
-        ("part", part_in, buf), ("toks", dy_in, toks), ("q", q_in, q), ("k", k_in, k),
+        ("toks", dy_in, toks), ("q", q_in, q), ("k", k_in, k),
         ("v", v_in, v), ("lse", lse_in, lse), ("att", att_in, att), ("w", wqkv_in, w),
-        ("down", sdown_in, down_out.at[:, spot(where), where[4]]),
+        ("down", sdown_in, down_out.at[:, spot(where), where[4]]), ("a1", a1_in, a1),
+        ("part", part_in, buf_down),
     ):
         loads.start(name, src, dst)
     greet(where, PEERS + REP_NEIGHBOURS)
-    down = Scatter(where, buf, land, *sems[0:2])
+    down = Scatter(where, buf_down, land_down, *sems[0:2])
     one = Scatter(where, buf, land, *sems[2:4])
     sum_qkv = [
         SlabScatter(where, gqkv, qkv_0, qkv_1, *sems[4:6]),
@@ -1200,15 +1301,12 @@
         ),
     ]
     back_down = RingGather(where, down_out, *sems[16:18])
-    back_out = RingGather(where, out_out, *sems[18:20])
+    back_out = SlabGather(where, out_out, *sems[18:20])
     vectors = Vectors(where, *sems[20:28])
     plan = Agenda()
     back_gu.begin()
-    loads.wait("part")
-    plan.add(agenda(down, TOKEN_TURNS, 0, 6, True))
-    plan.until(0.9)
     loads.wait("down")
-    plan.add(slab_agenda(back_down, 1, 5))
+    plan.add(slab_agenda(back_down, 1.5, 5))
     plan.until(1.5)
     loads.wait("toks")
 
@@ -1216,19 +1314,15 @@
     def _(i):
         da[chunk_rows(i), :] = dot_nt(token_chunk(toks, i), ow_ref[...]).astype(BF)
 
-    back_gu.middle()
-    plan.add(slab_agenda(back_gu, 5, 9))
-    plan.until(5)
-    loads.wait("q", "k", "v", "lse", "att")
-    left = att[...].astype(F32).T.astype(BF)
-    for n in range(4):
-        right = toks[:, :, n * 512 : (n + 1) * 512].reshape(TOTAL, 512)
-        gout[n] = dot(left, right).astype(BF).reshape(8, 2, SLAB, 512)
-    loads.start("a1", a1_in, toks)
-    plan.add([(7, sum_out, 0), (12, sum_out, 1), (30, sum_out, 2)])
-    plan.until(7.5)
-    attend_back(q, k, v, da, lse, kt, dqt, dk, dv, lambda i: plan.until(8.5 + 3 * i))
-    plan.until(23)
+    loads.wait("q", "k", "v", "lse")
+
+    def poll(i):
+        if i == 0:
+            back_gu.middle()
+            plan.add(slab_agenda(back_gu, 6, 9))
+        plan.until((6.5, 9, 12.5, 17)[i])
+
+    attend_back(q, k, v, da, lse, kt, dqt, dk, dv, poll)
     vectors.msg[...] = jnp.zeros_like(vectors.msg)
     for i in range(CHUNKS):
         rows = slice(i * CHUNK, (i + 1) * CHUNK)
@@ -1239,49 +1333,42 @@
             low = value.astype(BF)
             dqkv[rows, j * LOCAL : (j + 1) * LOCAL] = low
             vectors.msg[0, 4 + j : 5 + j, :] += jnp.sum(low.astype(F32), 0, keepdims=True)
-    plan.until(25)
-    loads.wait("a1", "w")
-    outer(toks, dqkv.at[:, pl.ds(0, HALF)], gqkv)
+    loads.wait("w")
+    times_back(dqkv, w, buf)
+    plan.add(agenda(one, 20))
+    plan.until(20.9)
+    loads.wait("a1")
+    for m in range(4):
+        outer(a1, dqkv.at[:, pl.ds(0, HALF)], gqkv, 2 * m, 2 * m + 2)
+        plan.until(22 + 1.3 * m)
     sum_qkv[0].turn(0)
-    plan.until(29)
-    outer(toks, dqkv.at[:, pl.ds(HALF, HALF)], gkv)
+    for m in range(4):
+        outer(a1, dqkv.at[:, pl.ds(HALF, HALF)], gkv, 2 * m, 2 * m + 2)
+        plan.until(27.3 + 1.3 * m)
     sum_qkv[1].turn(0)
-    plan.until(32)
     sum_qkv[0].turn(1)
-    down.finish()
-    for step in NEIGHBOURS:
-        pl.semaphore_signal(credit, inc=1, device_id=device(where, step), device_id_type=MESH)
-    act_ref[...] = (mid_ref[...] + buf[me].astype(F32)).astype(BF)
-    times_back(dqkv, w, buf)
+    plan.until(33)
+    loads.wait("att")
+    left = att[...].astype(F32).T.astype(BF)
+    for n in range(4):
+        right = toks[:, :, n * 512 : (n + 1) * 512].reshape(TOTAL, 512)
+        gout[n] = dot(left, right).astype(BF).reshape(8, 2, SLAB, 512)
+    sum_out.turn(0)
     sum_qkv[1].turn(1)
-    pl.semaphore_wait(credit, len(NEIGHBOURS))
-    plan.add(agenda(one, TOKEN_TURNS, 38, 5.5, True))
+    plan.until(36)
+    sum_out.turn(1)
+    back_down.finish()
     plan.until(40)
-    sum_out.close()
-    out_own = pltpu.make_async_copy(
-        sum_out.total(), out_out.at[:, spot(where), where[4]], own_sems.at[2]
-    )
-    out_own.start()
-    plan.until(44)
     sum_qkv[0].turn(2)
-    out_own.wait()
-    plan.add(slab_agenda(back_out, 44, 4))
-    plan.until(50)
+    back_gu.finish()
     sum_qkv[0].close()
     back_qkv[0].begin()
     sum_qkv[1].turn(2)
-    plan.until(53)
-    back_qkv[0].middle()
-    back_qkv[0].turn(0)
-    plan.until(55)
-    sum_qkv[1].close()
-    back_qkv[1].begin()
-    back_qkv[0].turn(1)
-    plan.until(58)
-    back_qkv[1].middle()
-    back_qkv[1].turn(0)
-    plan.until(62)
+    plan.until(1000)
     one.take_all()
+    loads.wait("part")
+    plan.add(agenda(down, 50))
+    plan.until(50.9)
     gain = small_row(small_ref, 0)
     _, scaled, inverse = normalize(x_ref[...].astype(F32), gain, small_row(small_ref, 1))
     grad = buf[me].astype(F32)
@@ -1294,19 +1381,47 @@
         if d:
             vectors.msg[d, 4:7, :] = vectors.msg[0, 4:7, :]
     vectors.begin()
+    grad_ref[...] = dmid_ref[...] + normalize_back(grad, gain, scaled, inverse)
+    sum_qkv[1].close()
+    back_qkv[1].begin()
+    back_qkv[0].middle()
+    back_qkv[0].turn(0)
+    plan.until(56)
+    vectors.middle()
+    back_qkv[0].turn(1)
+    plan.until(57)
+    back_qkv[1].middle()
+    back_qkv[1].turn(0)
+    vectors.round(0)
+    plan.until(59)
+    sum_out.turn(2)
     back_qkv[1].turn(1)
-    back_qkv[0].turn(2)
-    grad_ref[...] = dmid_ref[...] + normalize_back(grad, gain, scaled, inverse)
-    vectors.middle()
-    vectors.round(0)
     vectors.round(1)
+    one.settle()
+    sum_qkv[0].finish()
+    sum_out.close()
+    out_own = pltpu.make_async_copy(
+        sum_out.total(), out_out.at[:, spot(where), where[4]], own_sems.at[2]
+    )
+    out_own.start()
     vectors.round(2)
     vec_ref[...] = vectors.mine[3]
+    plan.until(65)
+    out_own.wait()
+    back_out.turn(0)
+    sum_qkv[1].finish()
     plan.until(1000)
+    back_qkv[0].turn(2)
+    back_out.turn(1)
+    sum_out.finish()
+    vectors.finish()
+    loads.finish()
     back_qkv[1].turn(2)
-    for mover in (one, *sum_qkv, sum_out, back_gu, back_down, back_out, *back_qkv, vectors):
+    down.take_all()
+    act_ref[...] = (mid_ref[...] + buf_down[me].astype(F32)).astype(BF)
+    back_out.turn(2)
+    for mover in (down, *back_qkv, back_out):
         mover.finish()
-    loads.finish()
 
 
 def back(x, mid, dmid, small, sums_two, table, out_weight, dy, a1, w_qkv, q, k, v, att, lse, s_gu, s_down, part_down):
@@ -1325,6 +1440,7 @@
         out_specs=(VM,) * 3 + (ANY,) * 5,
         scratch_shapes=[
             pltpu.VMEM(tokens, BF),
+            pltpu.VMEM(tokens, BF),
             pltpu.VMEM(QKV_SPAN, BF),
             *[pltpu.VMEM((TOTAL, LOCAL), BF)] * 4,
             pltpu.VMEM((8, TOTAL), F32),
@@ -1336,6 +1452,8 @@
             pltpu.VMEM((TOTAL, 3 * LOCAL), BF),
             pltpu.VMEM(tokens, BF),
             pltpu.VMEM((LANDINGS, ROWS, FAR_COLS), BF),
+            pltpu.VMEM(tokens, BF),
+            pltpu.VMEM((LANDINGS, ROWS, FAR_COLS), BF),
             pltpu.VMEM(HALF_SPAN, BF),
             pltpu.VMEM(HALF_SPAN, BF),
             pltpu.VMEM(OUT_SPAN, BF),
@@ -1344,7 +1462,6 @@
             *scatter_scratch(4, 512),
             DMA((10,)),
             DMA((4,)),
-            pltpu.SemaphoreType.REGULAR,
         ]
         + [DMA((COUNT,))] * 4
         + slab_sems * 2

time: 408 us -> 388 us (0.951)
  Pallas kernels: 394 us -> 374 us
    pallas_call x1, Pallas kernels: 109 us -> 93 us  [middle(): pl.pallas_call(middle_kernel, out_shape=(sds((ROWS, WIDTH), F32), sds((8,...]
    pallas_call x1, Pallas kernels: 136 us -> 132 us  [front(): pl.pallas_call(front_kernel, out_shape=(sds((GROUP, 8, LOCAL), F32), sds(...]
where the time goes in v3:
time: 388 us; the launch traced here: 381 us
  Pallas kernels  374 us (96%)
  local copies, waits for them, and re-layouts  5.1 us (1%)
    pallas_call x1, Pallas kernels, back(): pl.pallas_call(back_kernel, out_shape=(sds((ROWS, WIDTH), F32), sds((ROWS...  136 us
    pallas_call x1, Pallas kernels, front(): pl.pallas_call(front_kernel, out_shape=(sds((GROUP, 8, LOCAL), F32), sds(...  132 us
    pallas_call x1, Pallas kernels, middle(): pl.pallas_call(middle_kernel, out_shape=(sds((ROWS, WIDTH), F32), sds((8,...  93 us
    pallas_call x1, Pallas kernels, unpack(): pl.pallas_call(unpack_kernel, grid_spec=pltpu.PrefetchScalarGridSpec(num_...  12.9 us

profile of v3, /device:TPU:3, one launch (start us, length us, event | category | flops | bytes accessed | tf_op | source)
XLA Modules:
  0.0 380.6 jit_solution(1504078869637962932)
XLA Ops:
  0.7 0.7 convert_add_fusion
  1.4 0.6 reshape.58.small_ref
  2.0 131.6 %front.1 = (f32[8,8,256]{2,1,0:T(8,128)}, f32[128,2048]{1,0:T(8,128)}, bf16[8,128,2048]{2,1,0:T(8,128)(2,1)}, bf16[8,128,2048]{2,1,0:T(8,128)(2,1)}, bf16[8,128,...) custom-call(bf16[128,2048]{1,0:T(8,128)(2,1)} %bitcast.15, ...), custom_call_target="tpu_custom_call" | custom-call | tf_op jit(solution)/shard_map/front/pallas_call | solution.py:1095
  133.6 93.0 %middle.1 = (f32[128,2048]{1,0:T(8,128)}, f32[8,2048]{1,0:T(8,128)}, bf16[8,128,2048]{2,1,0:T(8,128)(2,1)}, bf16[8,16,1536]{2,1,0:T(8,128)(2,1)}, bf16[3,16,2048...) custom-call(f32[128,2048]{1,0:T(8,128)} %get-tuple-element.43.mid_ref, bf16[1,128,2048]{2,1,0:T(8,128)(2,1)} %gy_own.1, ...), custom_call_target="tpu_custom_call" | custom-call | tf_op jit(solution)/shard_map/middle/pallas_call | solution.py:1223
  226.6 136.3 %back.1 = (f32[128,2048]{1,0:T(8,128)}, bf16[128,2048]{1,0:T(8,128)(2,1)}, f32[8,256]{1,0:T(8,128)}, bf16[8,8,2,16,1536]{4,3,2,1,0:T(8,128)(2,1)}, bf16[3,8,2,16...) custom-call(bf16[128,2048]{1,0:T(8,128)(2,1)} %bitcast.16, ...), custom_call_target="tpu_custom_call" | custom-call | tf_op jit(solution)/shard_map/back/pallas_call | solution.py:1431
  362.9 0.7 slice.17
  363.6 1.4 fusion
  365.0 0.6 reshape.67
  365.6 0.0 copy-start.1
  365.6 0.0 copy-start
  365.6 12.9 %unpack.1 = (f32[256,5632]{1,0:T(8,128)}, f32[256,5632]{1,0:T(8,128)}, f32[256,6144]{1,0:T(8,128)}, f32[256,2048]{1,0:T(8,128)}, f32[704,2048]{1,0:T(8,128)}) custom-call(s32[1]{0:T(128)} %bitcast.5.odd_ref, bf16[8,256,1536]{2,1,0:T(8,128)(2,1)} %bitcast.13, bf16[8,256,384]{2,1,0:T(8,128)(2,1)} %bitcast.17, bf16[8,256,384]{2,1,0:T(8,128)(2,1)} %bitcast.18, ...), custom_call_target="tpu_custom_call" | custom-call | tf_op jit(solution)/shard_map/unpack/pallas_call | solution.py:1504
  378.6 0.0 copy-done.1
  378.6 0.8 copy.27
  379.4 0.0 copy-done
  379.4 1.0 copy.28
Async XLA Ops:
  365.6 12.9 %copy-start.1 = (bf16[128,2048]{1,0:T(8,128)(2,1)S(1)}, bf16[128,2048]{1,0:T(8,128)(2,1)}, u32[]{:S(2)}) copy-start(bf16[128,2048]{1,0:T(8,128)(2,1)} %get-tuple-element.61) | copy-start | bytes 1572868
  365.6 13.7 %copy-start = (f32[128,2048]{1,0:T(8,128)S(1)}, f32[128,2048]{1,0:T(8,128)}, u32[]{:S(2)}) copy-start(f32[128,2048]{1,0:T(8,128)} %get-tuple-element.62) | copy-start | bytes 3145732
